TPU v7x, 256 devices: a whole 4x4x8 slice. The times are simulated.
256 devices in a mesh: ep: 32 (over z, y), tp: 8 (over x, core).
Axes of the slice: x: 4, y: 4, z: 8, core: 2. Of those that a mesh axis runs over, the one named last changes fastest.
Arguments:
- tokens: bfloat16 [8192, 3584], P('ep'), may hold values from -6 to 6
- expert_ids: int32 [8192, 2], P('ep'), may hold values from 0 to 63, as said below
- routing_weights: float32 [8192, 2], P('ep'), may hold values from 0.2 to 1
- up_weight: bfloat16 [64, 3584, 3072], P('ep', None, 'tp'), may hold values from -0.09375 to 0.09375
- down_weight: bfloat16 [64, 3072, 3584], P('ep', 'tp'), may hold values from -0.109375 to 0.109375
Outputs:
- moe_output: bfloat16 [8192, 3584], P('ep', 'tp')
Inputs may be any that keep to these rules, and one draw needn't show every extreme that they name: `expert_ids`: A row names two different experts. Among the 256 rows of one ep index no expert is named by more than 10 rows, and one expert, the same for every ep index, is named by exactly 10 rows of every ep index.
All inputs are finite; a program needn't handle non-finite values.
Results may differ from a plain program's by a relative error of at most 0.019.
Values may be sent and summed in bfloat16 or wider, within the bound.
A program may use at most 128 MiB of HBM per device.

v0:
```python
import jax
import jax.numpy as jnp
from jax import lax
from jax.sharding import PartitionSpec as P

TOP = 2


def apply_experts(piece, up_weight, down_weight):
    raised = jnp.einsum("rked,edh->rkeh", piece, up_weight, preferred_element_type=jnp.float32)
    hidden = jax.nn.silu(raised).astype(jnp.bfloat16)
    partial_out = jnp.einsum(
        "rkeh,ehd->rked", hidden, down_weight, preferred_element_type=jnp.float32
    )
    return partial_out.astype(jnp.bfloat16)


def on_device(tokens, expert_ids, routing_weights, up_weight, down_weight):
    tok_count, width_d = tokens.shape
    local_experts = up_weight.shape[0]
    ep_count = lax.axis_size("ep")
    expert_total = local_experts * ep_count
    capacity = 5 * tok_count * TOP // (4 * expert_total)
    assign = expert_ids.reshape(-1)
    one_hot = (assign[:, None] == jnp.arange(expert_total, dtype=jnp.int32)[None, :]).astype(
        jnp.int32
    )
    earlier = jnp.cumsum(one_hot, axis=0) - one_hot
    within = jnp.sum(earlier * one_hot, axis=1)
    target_rank = assign // local_experts
    local_slot = assign % local_experts
    position = (target_rank * capacity + within) * local_experts + local_slot
    buffer_rows = local_experts * ep_count * capacity
    sources = jnp.arange(tok_count * TOP, dtype=jnp.int32) // TOP
    owners = jnp.full((buffer_rows,), tok_count, jnp.int32).at[position].set(sources)
    padded = jnp.concatenate([tokens, jnp.zeros((1, width_d), tokens.dtype)], 0)
    outgoing = padded[owners].reshape(ep_count, capacity, local_experts, width_d)
    partial_rows = apply_experts(
        lax.all_to_all(outgoing, "ep", split_axis=0, concat_axis=0, tiled=True),
        up_weight,
        down_weight,
    )
    returned = lax.all_to_all(partial_rows, "ep", split_axis=0, concat_axis=0, tiled=True).reshape(
        buffer_rows, width_d
    )
    gathered = returned[position].reshape(tok_count, TOP, width_d)
    gathered = lax.optimization_barrier(gathered).astype(jnp.float32)
    summed = lax.psum_scatter(gathered.astype(jnp.bfloat16), "tp", scatter_dimension=2, tiled=True)
    picked = lax.optimization_barrier(summed).astype(jnp.float32)
    mixed = jnp.sum(routing_weights[:, :, None] * picked, axis=1)
    return mixed.astype(jnp.bfloat16)


def solution(mesh):
    placed = (P("ep", None), P("ep", None), P("ep", None), P("ep", None, "tp"), P("ep", "tp", None))
    return jax.shard_map(
        on_device, mesh=mesh, in_specs=placed, out_specs=P("ep", "tp"), check_vma=False
    )
```

profile of v0, /device:TPU:2, one launch (start us, length us, event | category | flops | bytes accessed | tf_op | source)
XLA Modules:
  0.0 391.5 jit_solution(16132479321810400504)
XLA Ops:
  6.5 0.8 copy.34
  7.3 0.1 eq.31
  7.5 0.1 eq.27
  7.6 0.1 reshape.150
  7.8 1.2 reduce-window.6
  9.0 0.2 slice_reduce_fusion
  9.3 0.1 fusion.21
  9.5 2.4 scatter_custom_fusion
  11.9 1.6 concatenate.3
  13.6 5.2 %gather_fusion = bf16[640,3584]{1,0:T(8,128)(2,1)} fusion(bf16[257,3584]{1,0:T(8,128)(2,1)S(1)} %concatenate.3, s32[1024]{0:T(1024)S(1)} %pad_clamp_fusion.1), kind=kCustom, calls=%fused_computation | custom fusion | bytes 9177600 | tf_op jit(solution)/shard_map/gather | solution.py:37
  18.7 7.4 %reshape.152 = bf16[32,10,2,3584]{3,2,1,0:T(2,128)(2,1)} reshape(bf16[640,3584]{1,0:T(8,128)(2,1)} %gather_fusion) | data formatting | bytes 9175040 | tf_op jit(solution)/shard_map/reshape | solution.py:37
  26.1 116.8 %all_to_all.10 = bf16[32,10,2,3584]{3,2,1,0:T(2,128)(2,1)} all-to-all(bf16[32,10,2,3584]{3,2,1,0:T(2,128)(2,1)} %reshape.152), channel_id=1, replica_groups=mesh['ep'=32,'tp'=8] {'ep'}, dimensions={0} | all-to-all | bytes 9175040 | tf_op jit(solution)/shard_map/all_to_all | solution.py:39
  143.0 12.5 %fusion = bf16[32,10,2,3584]{3,0,1,2:T(8,128)(2,1)} fusion(bf16[2,384,3584]{2,1,0:T(8,128)(2,1)} %param.9, bf16[2,3584,384]{2,1,0:T(8,128)(2,1)} %param.8, bf16[32,10,2,3584]{3,2,1,0:T(2,128)(2,1)} %all_to_all.10), kind=kOutput, calls=%fused_computation.4 | convolution fusion | flops 3526737920 | bytes 20185088 | tf_op jit(solution)/shard_map/rkeh,ehd->rked/dot_general | solution.py:12
  155.4 9.2 %copy.39 = bf16[32,10,2,3584]{3,2,1,0:T(2,128)(2,1)} copy(bf16[32,10,2,3584]{3,0,1,2:T(8,128)(2,1)} %fusion) | data formatting | bytes 9175040 | tf_op jit(solution)/shard_map/convert_element_type | solution.py:15
  164.6 4.8 %all-to-all-start.1 = ((bf16[32,10,2,3584]{3,2,1,0:T(2,128)(2,1)}), bf16[32,10,2,3584]{3,2,1,0:T(2,128)(2,1)}, u32[]{:S(2)}, u32[]{:S(2)}) async-start(bf16[32,10,2,3584]{3,2,1,0:T(2,128)(2,1)} %copy.39), calls=%async_computation.1 | async-start | bytes 9175040 | tf_op jit(solution)/shard_map/all_to_all | solution.py:43
  169.5 0.3 all-reduce.4.cloned.1.call-start
  169.8 101.2 %all-to-all-done.1 = bf16[32,10,2,3584]{3,2,1,0:T(2,128)(2,1)} async-done(((bf16[32,10,2,3584]{3,2,1,0:T(2,128)(2,1)}), bf16[32,10,2,3584]{3,2,1,0:T(2,128)(2,1)}, u32[]{:S(2)}, u32[]{:S(2)}) %all-to-all-start.1) | async-done | bytes 4587552 | tf_op jit(solution)/shard_map/all_to_all | solution.py:43
  270.9 7.5 %reshape.153 = bf16[640,3584]{1,0:T(8,128)(2,1)} reshape(bf16[32,10,2,3584]{3,2,1,0:T(2,128)(2,1)} %all-to-all-done.1) | data formatting | bytes 9175040 | tf_op jit(solution)/shard_map/reshape | solution.py:43
  278.4 10.8 %gather_fusion.1 = bf16[512,3584]{1,0:T(8,128)(2,1)} fusion(bf16[640,3584]{1,0:T(8,128)(2,1)} %reshape.153, s32[1024]{0:T(1024)S(1)} %pad_clamp_fusion), kind=kCustom, calls=%fused_computation.1 | custom fusion | bytes 7342080 | tf_op jit(solution)/shard_map/gather | solution.py:46
  289.2 8.1 %reshape.154 = bf16[256,2,3584]{2,1,0:T(2,128)(2,1)} reshape(bf16[512,3584]{1,0:T(8,128)(2,1)} %gather_fusion.1) | data formatting | bytes 7340032 | tf_op jit(solution)/shard_map/reshape | solution.py:46
  297.3 0.0 copy-start.1
  297.3 0.0 copy-start
  297.3 13.6 %copy.40 = bf16[256,2,3584]{0,1,2:T(2,128)(2,1)} copy(bf16[256,2,3584]{2,1,0:T(2,128)(2,1)} %reshape.154) | data formatting | bytes 7340032 | tf_op jit(solution)/shard_map/optimization_barrier | solution.py:47
  310.9 0.0 all-reduce.4.cloned.1.call-update
  310.9 0.0 copy-done.1
  310.9 0.6 dynamic-slice
  312.1 70.4 %all-reduce.4.cloned.1.call-done = bf16[256,2,3584]{0,1,2:T(2,128)(2,1)} async-done(((bf16[256,2,3584]{0,1,2:T(2,128)(2,1)}), bf16[256,2,3584]{0,1,2:T(2,128)(2,1)}) %all-reduce.4.cloned.1.call-update) | async-done | bytes 3670032
  382.5 1.3 constant_dynamic-slice_fusion
  383.9 0.0 copy-done
  383.9 0.8 multiply_reduce_fusion
  (8 shorter events, 0.1 us)
Async XLA Ops:
  164.6 106.3 %all-to-all-start.1 = ((bf16[32,10,2,3584]{3,2,1,0:T(2,128)(2,1)}), bf16[32,10,2,3584]{3,2,1,0:T(2,128)(2,1)}, u32[]{:S(2)}, u32[]{:S(2)}) async-start(bf16[32,10,2,3584]{3,2,1,0:T(2,128)(2,1)} %copy.39), calls=%async_computation.1 | async-start | bytes 9175040 | tf_op jit(solution)/shard_map/all_to_all | solution.py:43
  169.5 213.1 %all-reduce.4.cloned.1.call-start = ((), (), s32[]{:S(2)}) async-start(), calls=%async_computation.2 | async-start | bytes 7340032
  297.3 13.6 %copy-start.1 = (u32[256]{0:T(256)S(1)}, u32[256]{0:T(256)}, u32[]{:S(2)}) copy-start(u32[256]{0:T(256)} %constant.64) | copy-start | bytes 3076
  297.3 86.6 %copy-start = (f32[256,2]{0,1:T(2,128)S(1)}, f32[256,2]{0,1:T(2,128)}, u32[]{:S(2)}) copy-start(f32[256,2]{0,1:T(2,128)} %param.7) | copy-start | bytes 6148
Sparse Core Ops, SparseCore 0:
  311.0 71.4 all-reduce.3
where the time goes:
time: 395 us; the launch traced here: 392 us
  waiting for transfers between devices  172 us (44%)
  blocking collectives  117 us (30%)
  local copies, waits for them, and re-layouts  69.1 us (17%)
  between operations  14.2 us (4%)
  matrix products  12.5 us (3%)
  starting transfers between devices  5.11 us (1%)
    all_to_all x1, blocking collectives, on_device(): lax.all_to_all(outgoing, 'ep', split_axis=0, concat_axis=0, tiled=True)  117 us
    all_to_all x1, waiting for transfers between devices, on_device(): lax.all_to_all(partial_rows, 'ep', split_axis=0, concat_axis=0, tiled=True)  101 us
    unnamed x2, waiting for transfers between devices  70.4 us
    optimization_barrier x1, local copies, waits for them, and re-layouts, on_device(): gathered = lax.optimization_barrier(gathered).astype(jnp.float32)  13.6 us
    dot_general x1, matrix products, apply_experts(): jnp.einsum('rkeh,ehd->rked', hidden, down_weight, preferred_element_type=...  12.5 us
    gather x1, local copies, waits for them, and re-layouts, on_device(): gathered = returned[position].reshape(tok_count, TOP, width_d)  10.8 us
    convert_element_type x1, local copies, waits for them, and re-layouts, apply_experts(): return partial_out.astype(jnp.bfloat16)  9.16 us
    reshape x1, local copies, waits for them, and re-layouts, on_device(): gathered = returned[position].reshape(tok_count, TOP, width_d)  8.13 us
  transfers between devices with their start and end apart: 2, of which 2 were waited for; matrix products, arithmetic and copies ran while one was open for 0% of the time, Pallas kernels for 0%

commit v1 on v0

v1 whole, which is shorter than its diff:
```python
import jax
import jax.numpy as jnp
from jax import lax
from jax.sharding import PartitionSpec as P

TOP = 2


def on_device(tokens, expert_ids, routing_weights, up_weight, down_weight):
    tok_count, width_d = tokens.shape
    local_experts = up_weight.shape[0]
    ep_count = lax.axis_size("ep")
    tp_count = lax.axis_size("tp")
    tp_at = lax.axis_index("tp")
    part_d = width_d // tp_count
    expert_total = local_experts * ep_count
    capacity = 5 * tok_count * TOP // (4 * expert_total)
    rows = expert_total * capacity
    assign = expert_ids.reshape(-1)
    one_hot = (assign[:, None] == jnp.arange(expert_total, dtype=jnp.int32)[None, :]).astype(
        jnp.int32
    )
    earlier = jnp.cumsum(one_hot, axis=0) - one_hot
    within = jnp.sum(earlier * one_hot, axis=1)
    position = (assign * capacity + within).reshape(tok_count, TOP)
    row_at = jnp.arange(rows, dtype=jnp.int32)
    place0 = position[:, 0][:, None] == row_at[None, :]
    place1 = position[:, 1][:, None] == row_at[None, :]
    sent = (place0 | place1).astype(jnp.bfloat16)
    block = lax.dynamic_slice_in_dim(tokens, tp_at * part_d, part_d, 1)
    outgoing = jnp.einsum(
        "tr,td->rd", sent, block, preferred_element_type=jnp.float32
    ).astype(jnp.bfloat16)
    outgoing = outgoing.reshape(ep_count, local_experts * capacity, part_d)
    arrived = lax.all_to_all(outgoing, "ep", split_axis=0, concat_axis=0, tiled=True)
    full = lax.all_gather(arrived, "tp", axis=0, tiled=False)
    full = full.reshape(tp_count, ep_count, local_experts, capacity, part_d)
    up = up_weight.reshape(local_experts, tp_count, part_d, up_weight.shape[2])
    raised = jnp.einsum("srekd,esdh->erkh", full, up, preferred_element_type=jnp.float32)
    hidden = jax.nn.silu(raised).astype(jnp.bfloat16)
    down = down_weight.reshape(local_experts, down_weight.shape[1], tp_count, part_d)
    partial_rows = jnp.einsum(
        "erkh,ehsd->srekd", hidden, down, preferred_element_type=jnp.float32
    ).astype(jnp.bfloat16)
    partial_rows = partial_rows.reshape(tp_count, rows, part_d)
    summed = lax.psum_scatter(partial_rows, "tp", scatter_dimension=0, tiled=False)
    returned = lax.all_to_all(
        summed.reshape(ep_count, local_experts * capacity, part_d),
        "ep",
        split_axis=0,
        concat_axis=0,
        tiled=True,
    ).reshape(rows, part_d)
    first = jnp.dot(place0.astype(jnp.bfloat16), returned, preferred_element_type=jnp.float32)
    second = jnp.dot(place1.astype(jnp.bfloat16), returned, preferred_element_type=jnp.float32)
    mixed = routing_weights[:, :1] * first + routing_weights[:, 1:] * second
    return mixed.astype(jnp.bfloat16)


def solution(mesh):
    placed = (P("ep", None), P("ep", None), P("ep", None), P("ep", None, "tp"), P("ep", "tp", None))
    return jax.shard_map(
        on_device, mesh=mesh, in_specs=placed, out_specs=P("ep", "tp"), check_vma=False
    )
```

time: 395 us -> 196 us (0.50)
  waiting for transfers between devices: 172 us -> 88.5 us
  blocking collectives: 117 us -> 34.2 us
  local copies, waits for them, and re-layouts: 69.1 us -> 30.6 us
  starting transfers between devices: 5.11 us -> 9.95 us
    all_to_all x1, blocking collectives: 117 us -> 34.2 us  [on_device(): lax.all_to_all(outgoing, 'ep', split_axis=0, concat_axis=0, tiled=True)]
    all_to_all x1, waiting for transfers between devices: 101 us -> 23.4 us  [on_device(): lax.all_to_all(summed.reshape(ep_count, local_experts * capacity, part_d)...]
    unnamed x2, waiting for transfers between devices: 70.4 us -> 0.03 us
    reduce_scatter x0 -> x1, waiting for transfers between devices: none -> 38.6 us  [on_device(): lax.psum_scatter(partial_rows, 'tp', scatter_dimension=0, tiled=False)]
    all_gather x0 -> x1, waiting for transfers between devices: none -> 26.5 us  [on_device(): full = lax.all_gather(arrived, 'tp', axis=0, tiled=False)]
    gather x2 -> x0, local copies, waits for them, and re-layouts: 15.9 us -> none  [the longest x1 10.8 us: on_device(): gathered = returned[position].reshape(tok_count, TOP, width_d)]
    reshape x4 -> x3, local copies, waits for them, and re-layouts: 23.2 us -> 9.28 us  [the longest x1 8.8 us: on_device(): partial_rows = partial_rows.reshape(tp_count, rows, part_d)]
    optimization_barrier x1 -> x0, local copies, waits for them, and re-layouts: 13.6 us -> none  [on_device(): gathered = lax.optimization_barrier(gathered).astype(jnp.float32)]
  transfers between devices with their start and end apart: 2 -> 3, of which waited for: 2 -> 3; matrix products, arithmetic and copies ran while one was open for 0% -> 4% of each run, Pallas kernels for 0% -> 0%
where the time goes in v1:
time: 196 us; the launch traced here: 194 us
  waiting for transfers between devices  88.5 us (45%)
  blocking collectives  34.2 us (17%)
  local copies, waits for them, and re-layouts  30.6 us (16%)
  matrix products  15.6 us (8%)
  between operations  13.5 us (7%)
  starting transfers between devices  9.95 us (5%)
  other arithmetic  2.08 us (1%)
    reduce_scatter x1, waiting for transfers between devices, on_device(): lax.psum_scatter(partial_rows, 'tp', scatter_dimension=0, tiled=False)  38.6 us
    all_to_all x1, blocking collectives, on_device(): lax.all_to_all(outgoing, 'ep', split_axis=0, concat_axis=0, tiled=True)  34.2 us
    all_gather x1, waiting for transfers between devices, on_device(): full = lax.all_gather(arrived, 'tp', axis=0, tiled=False)  26.5 us
    all_to_all x1, waiting for transfers between devices, on_device(): lax.all_to_all(summed.reshape(ep_count, local_experts * capacity, part_d)...  23.4 us
    dot_general x1, matrix products, on_device(): jnp.einsum('erkh,ehsd->srekd', hidden, down, preferred_element_type=jnp.f...  13.3 us
    all_to_all x1, starting transfers between devices, on_device(): lax.all_to_all(summed.reshape(ep_count, local_experts * capacity, part_d)...  9.91 us
    unnamed x6, local copies, waits for them, and re-layouts  9.23 us
    reshape x1, local copies, waits for them, and re-layouts, on_device(): partial_rows = partial_rows.reshape(tp_count, rows, part_d)  8.8 us
  transfers between devices with their start and end apart: 3, of which 3 were waited for; matrix products, arithmetic and copies ran while one was open for 4% of the time, Pallas kernels for 0%

profile of v1, /device:TPU:2, one launch (start us, length us, event | category | flops | bytes accessed | tf_op | source)
XLA Modules:
  0.0 194.5 jit_solution(18246150749148414935)
XLA Ops:
  6.5 0.0 copy-start
  6.5 0.0 all-gather.3.cloned.1.call-start
  6.5 0.9 copy.37
  7.5 0.1 eq.59
  7.6 0.1 eq.55
  7.8 1.2 reduce-window.6
  9.0 0.2 slice_reduce_fusion
  9.3 0.1 fusion.13
  9.4 0.1 reduce_sum.12
  9.6 0.1 copy.40
  9.6 0.7 multiply_add_fusion
  10.3 0.0 copy-done
  10.3 0.6 convolution_convert_fusion
  11.0 0.2 copy.41
  11.2 0.2 reshape.39
  11.4 34.2 %all_to_all.10 = bf16[32,20,448]{2,1,0:T(8,128)(2,1)S(1)} all-to-all(bf16[32,20,448]{2,1,0:T(8,128)(2,1)S(1)} %reshape.39), channel_id=1, replica_groups=mesh['ep'=32,'tp'=8] {'ep'}, dimensions={0} | all-to-all | bytes 1146880 | tf_op jit(solution)/shard_map/all_to_all | solution.py:35
  45.6 1.0 copy.42
  46.7 0.0 all-gather.3.cloned.1.call-update
  46.7 0.0 reduce-scatter.2.cloned.1.call-start
  46.7 8.3 %copy.43 = bf16[2,384,3584]{1,2,0:T(8,128)(2,1)} copy(bf16[2,384,3584]{2,1,0:T(8,128)(2,1)} %param.9) | data formatting | bytes 11010048 | tf_op args[4]
  55.0 26.5 %all-gather.3.cloned.1.call-done = bf16[256,20,448]{2,0,1:T(8,128)(2,1)} async-done(((bf16[32,20,448]{2,0,1:T(8,128)(2,1)}), bf16[256,20,448]{2,0,1:T(8,128)(2,1)}) %all-gather.3.cloned.1.call-update) | async-done | bytes 4587536 | tf_op jit(solution)/shard_map/all_gather | solution.py:36
  81.5 13.3 %convert_bitcast_fusion = bf16[8,32,2,10,448]{4,1,0,3,2:T(8,128)(2,1)} fusion(bf16[2,384,8,448,1]{1,3,2,4,0:T(8,128)(2,1)} %bitcast.58, bf16[8,32,2,10,448]{4,1,0,3,2:T(8,128)(2,1)} %bitcast.60, bf16[2,8,448,384,1]{3,2,1,4,0:T(8,128)(2,1)} %bitcast.57), kind=kOutput, calls=%fused_computation | convolution fusion | flops 3526737920 | bytes 20185088 | tf_op jit(solution)/shard_map/erkh,ehsd->srekd/dot_general | solution.py:42
  94.8 7.7 %copy.44 = bf16[8,32,2,10,448]{4,0,3,2,1:T(8,128)(2,1)} copy(bf16[8,32,2,10,448]{4,1,0,3,2:T(8,128)(2,1)} %convert_bitcast_fusion) | data formatting | bytes 9175040 | tf_op jit(solution)/shard_map/convert_element_type | solution.py:44
  102.5 8.8 %copy.45 = bf16[8,640,448]{1,2,0:T(8,128)(2,1)} copy(bf16[8,640,448]{2,0,1:T(8,128)(2,1)} %bitcast.59) | data formatting | bytes 9175040 | tf_op jit(solution)/shard_map/reshape | solution.py:45
  111.3 0.0 copy-start.1
  111.3 0.0 reduce-scatter.2.cloned.1.call-update
  111.4 38.6 %reduce-scatter.2.cloned.1.call-done = bf16[1,640,448]{1,2,0:T(8,128)(2,1)} async-done(((bf16[8,640,448]{1,2,0:T(8,128)(2,1)}), bf16[1,640,448]{1,2,0:T(8,128)(2,1)}) %reduce-scatter.2.cloned.1.call-update) | async-done | bytes 573456 | tf_op jit(solution)/shard_map/reduce_scatter | solution.py:46
  150.0 1.3 copy.46
  151.3 1.1 reshape_reduce_scatter.3
  152.3 9.9 %all-to-all-start.1 = ((bf16[32,20,448]{2,1,0:T(8,128)(2,1)}), bf16[32,20,448]{2,1,0:T(8,128)(2,1)S(1)}, u32[]{:S(2)}, u32[]{:S(2)}) async-start(bf16[32,20,448]{2,1,0:T(8,128)(2,1)} %reshape_reduce_scatter.3), calls=%async_computation.2 | async-start | bytes 1572864 | tf_op jit(solution)/shard_map/all_to_all | solution.py:47
  162.2 0.0 copy-done.1
  162.3 23.4 %all-to-all-done.1 = bf16[32,20,448]{2,1,0:T(8,128)(2,1)S(1)} async-done(((bf16[32,20,448]{2,1,0:T(8,128)(2,1)}), bf16[32,20,448]{2,1,0:T(8,128)(2,1)S(1)}, u32[]{:S(2)}, u32[]{:S(2)}) %all-to-all-start.1) | async-done | bytes 573472 | tf_op jit(solution)/shard_map/all_to_all | solution.py:47
  185.7 0.3 reshape.44
  186.0 0.5 convolution_multiply_fusion.1
  186.5 1.2 fusion.1
  (5 shorter events, 0.1 us)
Async XLA Ops:
  6.5 3.8 %copy-start = (bf16[256,3584]{1,0:T(8,128)(2,1)S(1)}, bf16[256,3584]{1,0:T(8,128)(2,1)}, u32[]{:S(2)}) copy-start(bf16[256,3584]{1,0:T(8,128)(2,1)} %param.5) | copy-start | bytes 5505028
  6.5 74.9 %all-gather.3.cloned.1.call-start = ((), (), s32[]{:S(2)}) async-start(), calls=%async_computation.4 | async-start | bytes 5898240 | tf_op jit(solution)/shard_map/all_gather | solution.py:36
  46.7 103.3 %reduce-scatter.2.cloned.1.call-start = ((), (), s32[]{:S(2)}) async-start(), calls=%async_computation.3 | async-start | bytes 5160960 | tf_op jit(solution)/shard_map/reduce_scatter | solution.py:46
  111.3 50.9 %copy-start.1 = (f32[256,2]{0,1:T(2,128)S(1)}, f32[256,2]{0,1:T(2,128)}, u32[]{:S(2)}) copy-start(f32[256,2]{0,1:T(2,128)} %param.7) | copy-start | bytes 6148
  152.3 33.3 %all-to-all-start.1 = ((bf16[32,20,448]{2,1,0:T(8,128)(2,1)}), bf16[32,20,448]{2,1,0:T(8,128)(2,1)S(1)}, u32[]{:S(2)}, u32[]{:S(2)}) async-start(bf16[32,20,448]{2,1,0:T(8,128)(2,1)} %reshape_reduce_scatter.3), calls=%async_computation.2 | async-start | bytes 1572864 | tf_op jit(solution)/shard_map/all_to_all | solution.py:47
Sparse Core Ops, SparseCore 0:
  46.8 34.6 all-gather.2
  111.5 38.4 reduce-scatter.1

commit v2 on v0

v2 whole, which is shorter than its diff:
```python
import jax
import jax.numpy as jnp
from jax import lax
from jax.experimental import pallas as pl
from jax.experimental.pallas import tpu as pltpu
from jax.sharding import PartitionSpec as P

MESH = pl.DeviceIdType.MESH
BF16 = jnp.bfloat16
F32 = jnp.float32

NZ, NY, NX, NC = 8, 4, 4, 2
TOP = 2
LOCAL = 2
CAP = 10
LANES = 128
TILES = 7
FIRST = 4
BLOCKS = 8
BROWS = 80
ROWS = BLOCKS * BROWS
HALF = BLOCKS // 2
OPP, RIGHT, LEFT, OWN = 0, 1, 2, 3


def kernel(
    ids_ref, rw_ref, tok_hbm, up_hbm, down_hbm, out_ref,
    tok, up, down, place, perm, mixw,
    gz, zb, yb, xb, raised, hid,
    part, other, cross, half_in, full_in, summed, yr, zo, zr, mid_in, mid_out,
    tok_sem, w_sem,
    zs, zr_sem, ys, yr_sem, xs, xr, cs, cr,
    rcs, rcr, rxs, rxr, rys, ryr, rzs, rzr, ms, mr,
):
    ep = lax.axis_index("ep")
    tp = lax.axis_index("tp")
    z, y = lax.div(ep, NY), lax.rem(ep, NY)
    x, c = lax.div(tp, NC), lax.rem(tp, NC)
    right, left, opp = lax.rem(x + 1, NX), lax.rem(x + 3, NX), lax.rem(x + 2, NX)
    twin = x * NC + (1 - c)
    right_id, left_id = right * NC + c, left * NC + c

    def tile(chip, j, core):
        return chip * TILES + core * FIRST + j

    def lanes(g):
        return pl.ds(pl.multiple_of(g * LANES, LANES), LANES)

    def push(src, dst, send, recv, to_ep, to_tp):
        return pltpu.make_async_remote_copy(
            src_ref=src, dst_ref=dst, send_sem=send, recv_sem=recv,
            device_id=(to_ep, to_tp), device_id_type=MESH,
        )

    def owned(j, body):
        if j < FIRST - 1:
            body()
        else:
            pl.when(c == 0)(body)

    barrier = pltpu.get_barrier_semaphore()

    def greet(to_ep, to_tp):
        pl.semaphore_signal(barrier, inc=1, device_id=(to_ep, to_tp), device_id_type=MESH)

    def greet_z(d, _):
        greet(lax.rem(z + d, NZ) * NY + y, tp)
        return 0

    def greet_y(d, _):
        greet(z * NY + lax.rem(y + d, NY), tp)
        return 0

    lax.fori_loop(1, NZ, greet_z, 0)
    lax.fori_loop(1, NY, greet_y, 0)
    greet(ep, right_id)
    greet(ep, left_id)
    greet(ep, twin)

    def tok_copy(j):
        return pltpu.make_async_copy(tok_hbm.at[:, lanes(tile(x, j, c))], tok.at[j], tok_sem.at[j])

    for j in range(FIRST):
        owned(j, lambda j=j: tok_copy(j).start())
    up_copy = pltpu.make_async_copy(up_hbm, up, w_sem.at[0])
    down_copy = pltpu.make_async_copy(down_hbm, down, w_sem.at[1])
    up_copy.start()
    down_copy.start()

    tokens = ids_ref.shape[1]
    experts = LOCAL * NZ * NY
    ids0, ids1 = ids_ref[0:1, :], ids_ref[1:2, :]
    named = lax.broadcasted_iota(jnp.int32, (experts, tokens), 0)
    hot0 = (named == ids0).astype(F32)
    hot1 = (named == ids1).astype(F32)
    before = (
        lax.broadcasted_iota(jnp.int32, (tokens, tokens), 0)
        < lax.broadcasted_iota(jnp.int32, (tokens, tokens), 1)
    ).astype(F32).astype(BF16)
    earlier = jnp.dot((hot0 + hot1).astype(BF16), before, preferred_element_type=F32)
    within0 = jnp.sum(hot0 * earlier, axis=0, keepdims=True).astype(jnp.int32)
    within1 = jnp.sum(hot1 * earlier, axis=0, keepdims=True).astype(jnp.int32)
    pos0 = ids0 * CAP + within0
    pos1 = ids1 * CAP + within1
    for b in range(BLOCKS):
        at = lax.broadcasted_iota(jnp.int32, (BROWS, tokens), 0) + b * BROWS
        hits = jnp.where(at == pos0, 1.0, 0.0) + jnp.where(at == pos1, 1.0, 0.0)
        place[b * BROWS:(b + 1) * BROWS, :] = hits.astype(BF16)

    pl.semaphore_wait(barrier, (NZ - 1) + (NY - 1) + 3)

    def z_copy(src, dst, send, recv, j, d):
        to = lax.rem(z + d, NZ)
        return push(src.at[j, to], dst.at[j, z], send.at[j, d], recv.at[j, d], to * NY + y, tp)

    def z_land(src, dst, send, recv, j, d):
        of = lax.rem(z + NZ - d, NZ)
        return push(src.at[j, of], dst.at[j, of], send.at[j, d], recv.at[j, d], ep, tp)

    def z_start(src, dst, send, recv, j):
        def one(d, _):
            z_copy(src, dst, send, recv, j, d).start()
            return 0

        lax.fori_loop(1, NZ, one, 0)
        dst[j, z] = src[j, z]

    def z_wait(src, dst, send, recv, j):
        def one(d, _):
            z_land(src, dst, send, recv, j, d).wait_recv()
            return 0

        lax.fori_loop(1, NZ, one, 0)

    def z_sent(src, dst, send, recv, j):
        def one(d, _):
            z_copy(src, dst, send, recv, j, d).wait_send()
            return 0

        lax.fori_loop(1, NZ, one, 0)

    def y_rows(at):
        return pl.ds(LOCAL * at, LOCAL)

    def y_copy(src, dst, send, recv, j, g, d):
        to = lax.rem(y + d, NY)
        return push(
            src.at[j, y_rows(to)], dst.at[g, y_rows(y)], send.at[j, d], recv.at[j, d],
            z * NY + to, tp,
        )

    def y_land(src, dst, send, recv, j, g, d):
        of = lax.rem(y + NY - d, NY)
        return push(
            src.at[j, y_rows(of)], dst.at[g, y_rows(of)], send.at[j, d], recv.at[j, d], ep, tp
        )

    def y_start(src, dst, send, recv, j, g):
        def one(d, _):
            y_copy(src, dst, send, recv, j, g, d).start()
            return 0

        lax.fori_loop(1, NY, one, 0)
        dst[g, y_rows(y)] = src[j, y_rows(y)]

    def y_wait(src, dst, send, recv, j, g):
        def one(d, _):
            y_land(src, dst, send, recv, j, g, d).wait_recv()
            return 0

        lax.fori_loop(1, NY, one, 0)

    def y_sent(src, dst, send, recv, j, g):
        def one(d, _):
            y_copy(src, dst, send, recv, j, g, d).wait_send()
            return 0

        lax.fori_loop(1, NY, one, 0)

    def as_blocks(v):
        return v.reshape(BLOCKS, BROWS, LANES)

    def as_rows(v):
        return v.reshape(ROWS, LANES)

    to_z = (gz, zb, zs, zr_sem)
    to_y = (yb, xb, ys, yr_sem)

    def gather(j):
        tok_copy(j).wait()
        rows = jnp.dot(place[...], tok[j], preferred_element_type=F32)
        gz[j] = as_blocks(rows.astype(BF16))
        z_start(*to_z, j)

    def turn(j):
        z_wait(*to_z, j)
        rows = jnp.dot(perm[...], as_rows(zb[j]), preferred_element_type=F32)
        yb[j] = as_blocks(rows.astype(BF16))
        y_start(*to_y, j, tile(x, j, c))

    low, high = pl.ds(0, HALF), pl.ds(HALF, HALF)

    def x_copy(j, kind):
        if kind == 0:
            src, to = xb.at[tile(x, j, c)], right_id
        elif kind == 1:
            src, to = xb.at[tile(x, j, c)], left_id
        elif kind == 2:
            src, to = xb.at[tile(left, j, c), low], right_id
        else:
            src, to = xb.at[tile(right, j, c), high], left_id
        return push(src, src, xs.at[j, kind], xr.at[j, kind], ep, to)

    def x_land(j, kind):
        if kind == 0:
            dst = xb.at[tile(left, j, c)]
        elif kind == 1:
            dst = xb.at[tile(right, j, c)]
        elif kind == 2:
            dst = xb.at[tile(opp, j, c), low]
        else:
            dst = xb.at[tile(opp, j, c), high]
        return push(dst, dst, xs.at[j, kind], xr.at[j, kind], ep, tp)

    chips = {OPP: opp, RIGHT: right, LEFT: left, OWN: x}

    def c_copy(j, kind):
        src = xb.at[tile(chips[kind], j, c)]
        return push(src, src, cs.at[j, kind], cr.at[j, kind], ep, twin)

    def c_land(j, kind):
        dst = xb.at[tile(chips[kind], j, 1 - c)]
        return push(dst, dst, cs.at[j, kind], cr.at[j, kind], ep, tp)

    def spread(j):
        y_wait(*to_y, j, tile(x, j, c))
        x_copy(j, 0).start()
        x_copy(j, 1).start()
        c_copy(j, OWN).start()

    def onward(j):
        x_land(j, 0).wait_recv()
        x_copy(j, 2).start()
        x_land(j, 1).wait_recv()
        x_copy(j, 3).start()
        c_copy(j, LEFT).start()
        c_copy(j, RIGHT).start()

    def last_hop(j):
        x_land(j, 2).wait_recv()
        x_land(j, 3).wait_recv()
        c_copy(j, OPP).start()

    def multiply(j):
        def landed():
            for kind in (OWN, LEFT, RIGHT, OPP):
                c_land(j, kind).wait_recv()

        if j < FIRST - 1:
            landed()
        else:
            pl.when(c == 1)(landed)
        tiles = [chip * TILES + j for chip in range(NX)]
        if j < FIRST - 1:
            tiles += [chip * TILES + FIRST + j for chip in range(NX)]
        for e in range(LOCAL):
            rows = jnp.concatenate(
                [
                    jnp.concatenate([xb[g, LOCAL * at + e] for at in range(NY)], axis=0)
                    for g in tiles
                ],
                axis=1,
            )
            weight = jnp.concatenate([up[e, g * LANES:(g + 1) * LANES, :] for g in tiles], axis=0)
            product = jnp.dot(rows, weight, preferred_element_type=F32)
            if j == 0:
                raised[e] = product
            elif j < FIRST - 1:
                raised[e] = raised[e] + product
            else:
                v = raised[e] + product
                hid[e] = (v / (1.0 + jnp.exp(-v))).astype(BF16)

    for j in range(FIRST):
        owned(j, lambda j=j: gather(j))

    for b in range(BLOCKS):
        row = lax.broadcasted_iota(jnp.int32, (BROWS, 1), 0) + b * BROWS
        block = lax.shift_right_logical(row * 205, 11)
        source = (
            (lax.bitwise_and(block, 7) * BLOCKS + lax.shift_right_logical(block, 3)) * CAP
            + row - block * CAP
        )
        column = lax.broadcasted_iota(jnp.int32, (BROWS, ROWS), 1)
        perm[b * BROWS:(b + 1) * BROWS, :] = jnp.where(column == source, 1.0, 0.0).astype(BF16)

    def do(step, j):
        owned(j, lambda: step(j))

    do(turn, 0)
    do(spread, 0)
    do(turn, 1)
    do(spread, 1)
    do(onward, 0)
    do(turn, 2)
    do(spread, 2)
    do(last_hop, 0)
    do(onward, 1)
    do(turn, 3)
    do(spread, 3)

    w0, w1 = rw_ref[0:1, :], rw_ref[1:2, :]
    for b in range(ROWS // LANES):
        at = lax.broadcasted_iota(jnp.int32, (LANES, tokens), 0) + b * LANES
        mix = jnp.where(at == pos0, w0, 0.0) + jnp.where(at == pos1, w1, 0.0)
        turned = jnp.transpose(mix)
        coarse = turned.astype(BF16)
        mixw[0:tokens, b * LANES:(b + 1) * LANES] = coarse
        mixw[tokens:, b * LANES:(b + 1) * LANES] = (turned - coarse.astype(F32)).astype(BF16)

    up_copy.wait()
    do(last_hop, 1)
    do(onward, 2)
    multiply(0)
    do(onward, 3)
    do(last_hop, 2)
    multiply(1)
    do(last_hop, 3)
    multiply(2)
    multiply(3)
    down_copy.wait()

    back_y = (summed, yr, rys, ryr)
    back_z = (zo, zr, rzs, rzr)

    def rc_copy(j, kind):
        return push(other.at[j, kind], cross.at[j, kind], rcs.at[j, kind], rcr.at[j, kind], ep, twin)

    def rx_copy(j, kind):
        if kind == 0:
            src, dst, to = part.at[j, OPP, low], half_in.at[j, 0], right_id
        elif kind == 1:
            src, dst, to = part.at[j, OPP, high], half_in.at[j, 1], left_id
        elif kind == 2:
            src, dst, to = part.at[j, RIGHT], full_in.at[j, 0], right_id
        else:
            src, dst, to = part.at[j, LEFT], full_in.at[j, 1], left_id
        return push(src, dst, rxs.at[j, kind], rxr.at[j, kind], ep, to)

    def rc_land(j, kind):
        dst = cross.at[j, kind]
        return push(dst, dst, rcs.at[j, kind], rcr.at[j, kind], ep, tp)

    def lower(j, kind):
        chip = chips[kind]
        for e in range(LOCAL):
            mine = down[e, :, lanes(tile(chip, j, c if j < FIRST - 1 else 0))]
            if j < FIRST - 1:
                theirs = down[e, :, lanes(tile(chip, j, 1 - c))]
                weight = jnp.concatenate([mine, theirs], axis=1)
            else:
                weight = mine
            product = jnp.dot(hid[e], weight, preferred_element_type=F32).astype(BF16)
            for at in range(NY):
                rows = product[at * BROWS:(at + 1) * BROWS]
                if j < FIRST - 1:
                    part[j, kind, LOCAL * at + e] = rows[:, :LANES]
                    other[j, kind, LOCAL * at + e] = rows[:, LANES:]
                else:
                    part[j, kind, LOCAL * at + e] = rows
        if j < FIRST - 1:
            rc_copy(j, kind).start()
        else:
            pl.when(c == 1)(lambda: extra_copy(kind).start())

    def extra_copy(kind):
        j = FIRST - 1
        return push(part.at[j, kind], cross.at[j, kind], rcs.at[j, kind], rcr.at[j, kind], ep, twin)

    def lower_all(j):
        for kind in (OPP, RIGHT, LEFT, OWN):
            lower(j, kind)

    def wide(v):
        return v.astype(F32)

    def add_opp(j):
        rc_land(j, OPP).wait_recv()
        part[j, OPP] = (wide(part[j, OPP]) + wide(cross[j, OPP])).astype(BF16)
        rx_copy(j, 0).start()
        rx_copy(j, 1).start()

    def add_sides(j):
        for kind, way, near, far in ((RIGHT, 0, low, high), (LEFT, 1, high, low)):
            rc_land(j, kind).wait_recv()
            part[j, kind, far] = (wide(part[j, kind, far]) + wide(cross[j, kind, far])).astype(BF16)
            rx_copy(j, way).wait_recv()
            part[j, kind, near] = (
                wide(part[j, kind, near]) + wide(cross[j, kind, near]) + wide(half_in[j, way])
            ).astype(BF16)
            rx_copy(j, 2 + way).start()

    def add_own(j):
        rc_land(j, OWN).wait_recv()
        rx_copy(j, 2).wait_recv()
        rx_copy(j, 3).wait_recv()
        summed[j] = (
            (wide(part[j, OWN]) + wide(cross[j, OWN]))
            + (wide(full_in[j, 0]) + wide(full_in[j, 1]))
        ).astype(BF16)
        y_start(*back_y, j, j)

    def turn_back(j):
        y_wait(*back_y, j, j)
        rows = jnp.dot(perm[...], as_rows(yr[j]), preferred_element_type=F32)
        zo[j] = as_blocks(rows.astype(BF16))
        z_start(*back_z, j)

    mid_copy = push(mid_out, mid_in, ms, mr, ep, twin)
    middle = LANES // 2

    def mix(j):
        z_wait(*back_z, j)
        both = jnp.dot(mixw[...], as_rows(zr[j]), preferred_element_type=F32)
        result = (both[:tokens] + both[tokens:]).astype(BF16)
        if j == FIRST - 1:
            mid_out[...] = result
            out_ref[:, j * LANES:j * LANES + middle] = result[:, :middle]
            mid_copy.start()
        else:
            def first():
                out_ref[:, j * LANES:(j + 1) * LANES] = result

            def second():
                out_ref[:, middle + j * LANES:middle + (j + 1) * LANES] = result

            pl.when(c == 0)(first)
            pl.when(c == 1)(second)

    order = (3, 0, 1, 2)
    a, b, d, e = order
    lower_all(a)
    do(add_opp, a)
    lower_all(b)
    do(add_sides, a)
    do(add_opp, b)
    lower_all(d)
    do(add_own, a)
    do(add_sides, b)
    do(add_opp, d)
    lower_all(e)
    do(turn_back, a)
    do(add_own, b)
    do(add_sides, d)
    do(add_opp, e)
    do(turn_back, b)
    do(add_own, d)
    do(add_sides, e)
    do(mix, a)
    do(turn_back, d)
    do(mix, b)
    do(add_own, e)
    do(mix, d)
    do(turn_back, e)

    def take_middle():
        mid_copy.wait_recv()
        out_ref[:, 0:middle] = mid_in[:, middle:]

    pl.when(c == 1)(take_middle)
    do(mix, e)

    def all_sent(j):
        z_sent(*to_z, j)
        y_sent(*to_y, j, tile(x, j, c))
        for kind in range(4):
            x_copy(j, kind).wait_send()
            c_copy(j, kind).wait_send()
            rx_copy(j, kind).wait_send()
            if j < FIRST - 1:
                rc_copy(j, kind).wait_send()
        y_sent(*back_y, j, j)
        z_sent(*back_z, j)

    for j in range(FIRST):
        do(all_sent, j)
    pl.when(c == 0)(lambda: mid_copy.wait_send())

    def extras_sent():
        for kind in range(4):
            extra_copy(kind).wait_send()

    pl.when(c == 1)(extras_sent)


def on_device(tokens, expert_ids, routing_weights, up_weight, down_weight):
    count, width = tokens.shape
    hidden = up_weight.shape[2]
    dma = pltpu.SemaphoreType.DMA
    blocks = (BLOCKS, BROWS, LANES)
    any_space = pl.BlockSpec(memory_space=pl.ANY)
    in_vmem = pl.BlockSpec(memory_space=pltpu.VMEM)
    per_z, per_y, by_kind = dma((FIRST, NZ)), dma((FIRST, NY)), dma((FIRST, 4))
    tile_set = pltpu.VMEM((FIRST,) + blocks, BF16)
    kind_set = pltpu.VMEM((FIRST, 4) + blocks, BF16)
    return pl.pallas_call(
        kernel,
        out_shape=jax.ShapeDtypeStruct((count, width // (NX * NC)), BF16),
        in_specs=[in_vmem, in_vmem, any_space, any_space, any_space],
        out_specs=in_vmem,
        scratch_shapes=[
            pltpu.VMEM((FIRST, count, LANES), BF16),
            pltpu.VMEM(up_weight.shape, BF16),
            pltpu.VMEM(down_weight.shape, BF16),
            pltpu.VMEM((ROWS, count), BF16),
            pltpu.VMEM((ROWS, ROWS), BF16),
            pltpu.VMEM((2 * count, ROWS), BF16),
            tile_set,
            tile_set,
            tile_set,
            pltpu.VMEM((NX * TILES,) + blocks, BF16),
            pltpu.VMEM((LOCAL, ROWS // LOCAL, hidden), F32),
            pltpu.VMEM((LOCAL, ROWS // LOCAL, hidden), BF16),
            kind_set,
            pltpu.VMEM((FIRST - 1, 4) + blocks, BF16),
            kind_set,
            pltpu.VMEM((FIRST, 2, HALF, BROWS, LANES), BF16),
            pltpu.VMEM((FIRST, 2) + blocks, BF16),
            tile_set,
            tile_set,
            tile_set,
            tile_set,
            pltpu.VMEM((count, LANES), BF16),
            pltpu.VMEM((count, LANES), BF16),
            dma((FIRST,)),
            dma((2,)),
            per_z, per_z, per_y, per_y, by_kind, by_kind, by_kind, by_kind,
            by_kind, by_kind, by_kind, by_kind, per_y, per_y, per_z, per_z, dma, dma,
        ],
        compiler_params=pltpu.CompilerParams(
            collective_id=0, has_side_effects=True, vmem_limit_bytes=60 * 1024 * 1024
        ),
        cost_estimate=pl.CostEstimate(
            flops=4 * ROWS * width * hidden, bytes_accessed=8 * width * hidden, transcendentals=0
        ),
        name="experts",
    )(expert_ids.T, routing_weights.T, tokens, up_weight, down_weight)


def solution(mesh):
    placed = (P("ep", None), P("ep", None), P("ep", None), P("ep", None, "tp"), P("ep", "tp", None))
    return jax.shard_map(
        on_device, mesh=mesh, in_specs=placed, out_specs=P("ep", "tp"), check_vma=False
    )
```

time: 395 us -> 100 us (0.25)
  waiting for transfers between devices: 172 us -> 0 us
  blocking collectives: 117 us -> 0 us
  Pallas kernels: 0 us -> 98.2 us
  local copies, waits for them, and re-layouts: 69.1 us -> 1.78 us
  between operations: 14.2 us -> 0.01 us
  matrix products: 12.5 us -> 0 us
  starting transfers between devices: 5.11 us -> 0 us
    all_to_all x1 -> x0, blocking collectives: 117 us -> none  [on_device(): lax.all_to_all(outgoing, 'ep', split_axis=0, concat_axis=0, tiled=True)]
    all_to_all x1 -> x0, waiting for transfers between devices: 101 us -> none  [on_device(): lax.all_to_all(partial_rows, 'ep', split_axis=0, concat_axis=0, tiled=True)]
    pallas_call x0 -> x1, Pallas kernels: none -> 98.2 us  [on_device(): pl.pallas_call(kernel, out_shape=jax.ShapeDtypeStruct((count, width // (N...]
    unnamed x2 -> x0, waiting for transfers between devices: 70.4 us -> none
    reshape x4 -> x0, local copies, waits for them, and re-layouts: 23.2 us -> none  [the longest x1 8.13 us: on_device(): gathered = returned[position].reshape(tok_count, TOP, width_d)]
    gather x2 -> x0, local copies, waits for them, and re-layouts: 15.9 us -> none  [the longest x1 10.8 us: on_device(): gathered = returned[position].reshape(tok_count, TOP, width_d)]
    optimization_barrier x1 -> x0, local copies, waits for them, and re-layouts: 13.6 us -> none  [on_device(): gathered = lax.optimization_barrier(gathered).astype(jnp.float32)]
    dot_general x1 -> x0, matrix products: 12.5 us -> none  [apply_experts(): jnp.einsum('rkeh,ehd->rked', hidden, down_weight, preferred_element_type=...]
  transfers between devices with their start and end apart: 2 -> 0, of which waited for: 2 -> 0; matrix products, arithmetic and copies ran while one was open for 0% -> 0% of each run, Pallas kernels for 0% -> 0%
where the time goes in v2:
time: 100 us; the launch traced here: 99.9 us
  Pallas kernels  98.2 us (98%)
  local copies, waits for them, and re-layouts  1.78 us (2%)
    pallas_call x1, Pallas kernels, on_device(): pl.pallas_call(kernel, out_shape=jax.ShapeDtypeStruct((count, width // (N...  98.2 us

profile of v2, /device:TPU:2, one launch (start us, length us, event | category | flops | bytes accessed | tf_op | source)
XLA Modules:
  0.0 99.9 jit_solution(13217722355601172838)
XLA Ops:
  0.0 98.2 %experts.1 = bf16[256,448]{1,0:T(8,128)(2,1)} custom-call(s32[2,256]{1,0:T(2,128)} %bitcast.2, f32[2,256]{1,0:T(2,128)} %bitcast.3, bf16[256,3584]{1,0:T(8,128)(2,1)} %tok_hbm.1, bf16[2,3584,384]{2,1,0:T(8,128)(2,1)} %up_hbm.1, bf16[2,384,3584]{2,1,0:T(8,128)(2,1)} %down_hbm.1), custom_call_target="tpu_custom_call" | custom-call | flops 3523215360 | bytes 11010048 | tf_op jit(solution)/shard_map/experts/pallas_call | solution.py:506
  98.2 1.8 %copy.6 = bf16[256,448]{0,1:T(8,128)(2,1)} copy(bf16[256,448]{1,0:T(8,128)(2,1)} %experts.1) | data formatting | bytes 458752 | tf_op jit(solution)/shard_map/experts/pallas_call | solution.py:506

commit v3 on v2

v3 whole, which is shorter than its diff:
```python
import jax
import jax.numpy as jnp
from jax import lax
from jax.experimental import pallas as pl
from jax.experimental.pallas import tpu as pltpu
from jax.sharding import PartitionSpec as P

MESH = pl.DeviceIdType.MESH
BF16 = jnp.bfloat16
F32 = jnp.float32

NZ, NY, NX, NC = 8, 4, 4, 2
TOP = 2
LOCAL = 2
CAP = 10
LANES = 128
TILES = 7
FIRST = 4
BLOCKS = 8
BROWS = 80
ROWS = BLOCKS * BROWS
HALF = BLOCKS // 2
OPP, RIGHT, LEFT, OWN = 0, 1, 2, 3
FIRST_UP, LAST_UP = (3, 3), (1, 1)


def kernel(
    ids_hbm, rw_hbm, tok_hbm, up_hbm, down_hbm, out_ref,
    ids_ref, rw_ref, tok, up, down, place, perm, mixw,
    gz, zb, yb, xb, raised, hid,
    part, other, cross, half_in, full_in, summed, yr, zo, zr, mid_in, mid_out,
    tok_sem, w_sem,
    zs, zr_sem, ys, yr_sem, xs, xr, cs, cr,
    rcs, rcr, rxs, rxr, rys, ryr, rzs, rzr, ms, mr,
):
    ep = lax.axis_index("ep")
    tp = lax.axis_index("tp")
    z, y = lax.div(ep, NY), lax.rem(ep, NY)
    x, c = lax.div(tp, NC), lax.rem(tp, NC)
    right, left, opp = lax.rem(x + 1, NX), lax.rem(x + 3, NX), lax.rem(x + 2, NX)
    twin = x * NC + (1 - c)
    right_id, left_id = right * NC + c, left * NC + c

    def tile(chip, j, core):
        return chip * TILES + core * FIRST + j

    def lanes(g):
        return pl.ds(pl.multiple_of(g * LANES, LANES), LANES)

    def push(src, dst, send, recv, to_ep, to_tp):
        return pltpu.make_async_remote_copy(
            src_ref=src, dst_ref=dst, send_sem=send, recv_sem=recv,
            device_id=(to_ep, to_tp), device_id_type=MESH,
        )

    def owned(j, body):
        if j < FIRST - 1:
            body()
        else:
            pl.when(c == 0)(body)

    barrier = pltpu.get_barrier_semaphore()

    def greet(to_ep, to_tp):
        pl.semaphore_signal(barrier, inc=1, device_id=(to_ep, to_tp), device_id_type=MESH)

    def greet_z(d, _):
        greet(lax.rem(z + d, NZ) * NY + y, tp)
        return 0

    def greet_y(d, _):
        greet(z * NY + lax.rem(y + d, NY), tp)
        return 0

    lax.fori_loop(1, NZ, greet_z, 0)
    lax.fori_loop(1, NY, greet_y, 0)
    greet(ep, right_id)
    greet(ep, left_id)
    greet(ep, twin)

    ids_copy = pltpu.make_async_copy(ids_hbm, ids_ref, w_sem.at[2])
    rw_copy = pltpu.make_async_copy(rw_hbm, rw_ref, w_sem.at[3])
    ids_copy.start()
    rw_copy.start()

    def tok_copy(j):
        return pltpu.make_async_copy(tok_hbm.at[:, lanes(tile(x, j, c))], tok.at[j], tok_sem.at[j])

    for j in range(FIRST):
        owned(j, lambda j=j: tok_copy(j).start())
    up_copy = pltpu.make_async_copy(up_hbm, up, w_sem.at[0])
    down_copy = pltpu.make_async_copy(down_hbm, down, w_sem.at[1])
    up_copy.start()
    down_copy.start()

    tokens = ids_ref.shape[1]
    experts = LOCAL * NZ * NY
    ids_copy.wait()
    ids0, ids1 = ids_ref[0:1, :], ids_ref[1:2, :]
    named = lax.broadcasted_iota(jnp.int32, (experts, tokens), 0)
    hot0 = (named == ids0).astype(F32)
    hot1 = (named == ids1).astype(F32)
    before = (
        lax.broadcasted_iota(jnp.int32, (tokens, tokens), 0)
        < lax.broadcasted_iota(jnp.int32, (tokens, tokens), 1)
    ).astype(F32).astype(BF16)
    earlier = jnp.dot((hot0 + hot1).astype(BF16), before, preferred_element_type=F32)
    within0 = jnp.sum(hot0 * earlier, axis=0, keepdims=True).astype(jnp.int32)
    within1 = jnp.sum(hot1 * earlier, axis=0, keepdims=True).astype(jnp.int32)
    pos0 = ids0 * CAP + within0
    pos1 = ids1 * CAP + within1
    for b in range(BLOCKS):
        at = lax.broadcasted_iota(jnp.int32, (BROWS, tokens), 0) + b * BROWS
        hits = jnp.where(at == pos0, 1.0, 0.0) + jnp.where(at == pos1, 1.0, 0.0)
        place[b * BROWS:(b + 1) * BROWS, :] = hits.astype(BF16)

    pl.semaphore_wait(barrier, (NZ - 1) + (NY - 1) + 3)

    def z_copy(src, dst, send, recv, j, d):
        to = lax.rem(z + d, NZ)
        return push(src.at[j, to], dst.at[j, z], send.at[j, d], recv.at[j, d], to * NY + y, tp)

    def z_land(src, dst, send, recv, j, d):
        of = lax.rem(z + NZ - d, NZ)
        return push(src.at[j, of], dst.at[j, of], send.at[j, d], recv.at[j, d], ep, tp)

    def z_start(src, dst, send, recv, j):
        def one(d, _):
            z_copy(src, dst, send, recv, j, d).start()
            return 0

        lax.fori_loop(1, NZ, one, 0)
        dst[j, z] = src[j, z]

    def z_wait(src, dst, send, recv, j):
        def one(d, _):
            z_land(src, dst, send, recv, j, d).wait_recv()
            return 0

        lax.fori_loop(1, NZ, one, 0)

    def z_sent(src, dst, send, recv, j):
        def one(d, _):
            z_copy(src, dst, send, recv, j, d).wait_send()
            return 0

        lax.fori_loop(1, NZ, one, 0)

    def y_rows(at):
        return pl.ds(LOCAL * at, LOCAL)

    def as_blocks(v):
        return v.reshape(BLOCKS, BROWS, LANES)

    def as_rows(v):
        return v.reshape(ROWS, LANES)

    def quarter(q):
        return pl.ds(LOCAL * q, LOCAL)

    def half(h):
        return pl.ds(HALF * h, HALF)

    to_z = (gz, zb, zs, zr_sem)

    def y_copy(j, d):
        to = lax.rem(y + d, NY)
        return push(
            yb.at[j, y_rows(to)], xb.at[tile(x, j, c), quarter(d)], ys.at[j, d], yr_sem.at[j, d],
            z * NY + to, tp,
        )

    def x_copy(j, q, way):
        if way == 0:
            src, to = xb.at[tile(x, j, c), quarter(q)], right_id
        elif way == 1:
            src, to = xb.at[tile(x, j, c), quarter(q)], left_id
        elif q % 2 == 0:
            src, to = xb.at[tile(left, j, c), quarter(q)], right_id
        else:
            src, to = xb.at[tile(right, j, c), quarter(q)], left_id
        return push(src, src, xs.at[j, way * NY + q], xr.at[j, way * NY + q], ep, to)

    def x_land(j, q, way):
        chip = (left, right, opp)[way]
        dst = xb.at[tile(chip, j, c), quarter(q)]
        return push(dst, dst, xs.at[j, way * NY + q], xr.at[j, way * NY + q], ep, tp)

    chips = {OPP: opp, RIGHT: right, LEFT: left, OWN: x}

    def c_copy(j, h, kind):
        src = xb.at[tile(chips[kind], j, c), half(h)]
        return push(src, src, cs.at[j, 4 * h + kind], cr.at[j, 4 * h + kind], ep, twin)

    def c_land(j, h, kind):
        dst = xb.at[tile(chips[kind], j, 1 - c), half(h)]
        return push(dst, dst, cs.at[j, 4 * h + kind], cr.at[j, 4 * h + kind], ep, tp)

    def gather(j):
        tok_copy(j).wait()
        rows = jnp.dot(place[...], tok[j], preferred_element_type=F32)
        gz[j] = as_blocks(rows.astype(BF16))
        z_start(*to_z, j)

    def spread(j, q):
        x_copy(j, q, 0).start()
        x_copy(j, q, 1).start()

    def turn(j):
        z_wait(*to_z, j)
        rows = jnp.dot(perm[...], as_rows(zb[j]), preferred_element_type=F32)
        yb[j] = as_blocks(rows.astype(BF16))
        for d in (2, 1, 3):
            y_copy(j, d).start()
        xb[tile(x, j, c), quarter(0)] = yb[j, y_rows(y)]
        spread(j, 0)

    def side(j, q):
        y_copy(j, q).wait_recv()
        spread(j, q)
        if q < 3:
            c_copy(j, q // 2, OWN).start()

    def forward(j, q):
        x_land(j, q, q % 2).wait_recv()
        x_copy(j, q, 2).start()

    def pass_left(j, h):
        x_land(j, 2 * h + 1, 0).wait_recv()
        c_copy(j, h, LEFT).start()

    def pass_right(j, h):
        x_land(j, 2 * h, 1).wait_recv()
        c_copy(j, h, RIGHT).start()

    def last_hop(j, h):
        x_land(j, 2 * h, 2).wait_recv()
        x_land(j, 2 * h + 1, 2).wait_recv()
        c_copy(j, h, OPP).start()

    def multiply(j, h):
        def landed():
            for kind in (OWN, LEFT, RIGHT, OPP):
                c_land(j, h, kind).wait_recv()

        if j < FIRST - 1:
            landed()
        else:
            pl.when(c == 1)(landed)
        tiles = [chip * TILES + j for chip in range(NX)]
        if j < FIRST - 1:
            tiles += [chip * TILES + FIRST + j for chip in range(NX)]
        for e in range(LOCAL):
            rows = jnp.concatenate(
                [
                    jnp.concatenate([xb[g, LOCAL * q + e] for q in (2 * h, 2 * h + 1)], axis=0)
                    for g in tiles
                ],
                axis=1,
            )
            weight = jnp.concatenate([up[e, g * LANES:(g + 1) * LANES, :] for g in tiles], axis=0)
            product = jnp.dot(rows, weight, preferred_element_type=F32)
            if j == FIRST_UP[h]:
                raised[h, e] = product
            elif j != LAST_UP[h]:
                raised[h, e] = raised[h, e] + product
            else:
                v = raised[h, e] + product
                hid[h, e] = (v / (1.0 + jnp.exp(-v))).astype(BF16)

    def make_perm():
        for b in range(BLOCKS):
            row = lax.broadcasted_iota(jnp.int32, (BROWS, 1), 0) + b * BROWS
            block = lax.shift_right_logical(row * 205, 11)
            source = (
                (lax.bitwise_and(block, 7) * BLOCKS + lax.shift_right_logical(block, 3)) * CAP
                + row - block * CAP
            )
            column = lax.broadcasted_iota(jnp.int32, (BROWS, ROWS), 1)
            perm[b * BROWS:(b + 1) * BROWS, :] = jnp.where(column == source, 1.0, 0.0).astype(BF16)

    def make_mix():
        rw_copy.wait()
        w0, w1 = rw_ref[0:1, :], rw_ref[1:2, :]
        for b in range(BLOCKS):
            at = lax.broadcasted_iota(jnp.int32, (BROWS, tokens), 0) + b * BROWS
            mix = jnp.where(at == pos0, w0, 0.0) + jnp.where(at == pos1, w1, 0.0)
            coarse = mix.astype(BF16)
            mixw[b * BROWS:(b + 1) * BROWS, 0:tokens] = coarse
            mixw[b * BROWS:(b + 1) * BROWS, tokens:] = (mix - coarse.astype(F32)).astype(BF16)

    back_z = (zo, zr, rzs, rzr)

    def rc_copy(j, h, kind):
        src = (other if j < FIRST - 1 else part).at[j, kind, half(h)]
        at = 4 * h + kind
        return push(src, cross.at[j, kind, half(h)], rcs.at[j, at], rcr.at[j, at], ep, twin)

    def rc_land(j, h, kind):
        dst = cross.at[j, kind, half(h)]
        at = 4 * h + kind
        return push(dst, dst, rcs.at[j, at], rcr.at[j, at], ep, tp)

    def rx_copy(j, h, kind):
        if kind == 0:
            src, dst, to = part.at[j, OPP, quarter(2 * h)], half_in.at[j, h, 0], right_id
        elif kind == 1:
            src, dst, to = part.at[j, OPP, quarter(2 * h + 1)], half_in.at[j, h, 1], left_id
        elif kind == 2:
            src, dst, to = part.at[j, RIGHT, half(h)], full_in.at[j, 0, half(h)], right_id
        else:
            src, dst, to = part.at[j, LEFT, half(h)], full_in.at[j, 1, half(h)], left_id
        at = 4 * h + kind
        return push(src, dst, rxs.at[j, at], rxr.at[j, at], ep, to)

    def ry_copy(j, d):
        to = lax.rem(y + NY - d, NY)
        return push(
            summed.at[j, quarter(d)], yr.at[j, y_rows(y)], rys.at[j, d], ryr.at[j, d],
            z * NY + to, tp,
        )

    def ry_land(j, d):
        dst = yr.at[j, y_rows(lax.rem(y + d, NY))]
        return push(dst, dst, rys.at[j, d], ryr.at[j, d], ep, tp)

    def lower(j, h, kind):
        chip = chips[kind]
        for e in range(LOCAL):
            mine = down[e, :, lanes(tile(chip, j, c if j < FIRST - 1 else 0))]
            if j < FIRST - 1:
                theirs = down[e, :, lanes(tile(chip, j, 1 - c))]
                weight = jnp.concatenate([mine, theirs], axis=1)
            else:
                weight = mine
            product = jnp.dot(hid[h, e], weight, preferred_element_type=F32).astype(BF16)
            for i in range(2):
                at = LOCAL * (2 * h + i) + e
                rows = product[i * BROWS:(i + 1) * BROWS]
                if j < FIRST - 1:
                    part[j, kind, at] = rows[:, :LANES]
                    other[j, kind, at] = rows[:, LANES:]
                else:
                    part[j, kind, at] = rows
        if j < FIRST - 1:
            rc_copy(j, h, kind).start()
        else:
            pl.when(c == 1)(lambda: rc_copy(j, h, kind).start())

    def wide(v):
        return v.astype(F32)

    def add_opp(j, h):
        rc_land(j, h, OPP).wait_recv()
        at = half(h)
        part[j, OPP, at] = (wide(part[j, OPP, at]) + wide(cross[j, OPP, at])).astype(BF16)
        rx_copy(j, h, 0).start()
        rx_copy(j, h, 1).start()

    def add_side(j, h, kind):
        way = 0 if kind == RIGHT else 1
        near, far = quarter(2 * h + way), quarter(2 * h + 1 - way)
        rc_land(j, h, kind).wait_recv()
        part[j, kind, far] = (wide(part[j, kind, far]) + wide(cross[j, kind, far])).astype(BF16)
        rx_copy(j, h, way).wait_recv()
        part[j, kind, near] = (
            wide(part[j, kind, near]) + wide(cross[j, kind, near]) + wide(half_in[j, h, way])
        ).astype(BF16)
        rx_copy(j, h, 2 + way).start()

    def add_own(j, h):
        rc_land(j, h, OWN).wait_recv()
        rx_copy(j, h, 2).wait_recv()
        rx_copy(j, h, 3).wait_recv()
        at = half(h)
        summed[j, at] = (
            (wide(part[j, OWN, at]) + wide(cross[j, OWN, at]))
            + (wide(full_in[j, 0, at]) + wide(full_in[j, 1, at]))
        ).astype(BF16)
        if h == 0:
            ry_copy(j, 1).start()
            yr[j, y_rows(y)] = summed[j, quarter(0)]
        else:
            ry_copy(j, 2).start()
            ry_copy(j, 3).start()

    def turn_back(j):
        for d in (1, 2, 3):
            ry_land(j, d).wait_recv()
        rows = jnp.dot(perm[...], as_rows(yr[j]), preferred_element_type=F32)
        zo[j] = as_blocks(rows.astype(BF16))
        z_start(*back_z, j)

    mid_copy = push(mid_out, mid_in, ms, mr, ep, twin)
    middle = LANES // 2

    def mix(j):
        z_wait(*back_z, j)
        both = lax.dot_general(
            as_rows(zr[j]), mixw[...], (((0,), (0,)), ((), ())), preferred_element_type=F32
        )
        result = (both[:, :tokens] + both[:, tokens:]).astype(BF16)
        if j == FIRST - 1:
            out_ref[j * LANES:j * LANES + middle, :] = result[:middle]
            mid_out[...] = result[middle:]
            mid_copy.start()
        else:
            def first():
                out_ref[j * LANES:(j + 1) * LANES, :] = result

            def second():
                out_ref[middle + j * LANES:middle + (j + 1) * LANES, :] = result

            pl.when(c == 0)(first)
            pl.when(c == 1)(second)

    def take_middle():
        mid_copy.wait_recv()
        out_ref[0:middle, :] = mid_in[...]

    def do(step, j, *h):
        owned(j, lambda: step(j, *h))

    do(gather, 3)
    do(gather, 0)
    do(gather, 2)
    do(gather, 1)
    make_perm()
    do(turn, 3)
    do(turn, 0)
    do(side, 3, 3)
    do(side, 3, 1)
    do(side, 3, 2)
    do(turn, 2)
    do(side, 0, 3)
    do(side, 0, 2)
    do(side, 0, 1)
    do(turn, 1)
    do(side, 2, 1)
    do(forward, 0, 0)
    do(side, 2, 3)
    do(forward, 0, 1)
    do(forward, 3, 1)
    do(forward, 3, 0)
    do(pass_left, 0, 0)
    do(side, 2, 2)
    do(side, 1, 1)
    do(pass_left, 3, 0)
    do(side, 1, 3)
    do(forward, 2, 1)
    do(forward, 2, 0)
    do(side, 1, 2)
    do(pass_right, 2, 0)
    do(last_hop, 3, 0)
    do(forward, 1, 0)
    do(forward, 1, 1)
    do(pass_right, 0, 0)
    do(forward, 3, 2)
    do(forward, 3, 3)
    make_mix()
    do(forward, 2, 2)
    do(forward, 2, 3)
    do(pass_left, 2, 0)
    do(pass_right, 3, 0)
    do(forward, 0, 2)
    do(last_hop, 0, 0)
    do(pass_left, 0, 1)
    do(pass_right, 3, 1)
    do(forward, 0, 3)
    do(pass_right, 0, 1)
    do(forward, 1, 3)
    do(pass_left, 3, 1)
    do(pass_left, 1, 0)
    do(pass_right, 1, 0)
    do(pass_left, 2, 1)
    do(last_hop, 2, 0)
    up_copy.wait()
    multiply(3, 0)
    do(forward, 1, 2)
    do(pass_right, 1, 1)
    do(last_hop, 1, 0)
    do(pass_right, 2, 1)
    multiply(0, 0)
    multiply(2, 0)
    do(last_hop, 3, 1)
    do(pass_left, 1, 1)
    multiply(1, 0)
    down_copy.wait()
    lower(3, 0, OPP)
    do(last_hop, 2, 1)
    lower(0, 0, OPP)
    lower(1, 0, OPP)
    lower(2, 0, OPP)
    multiply(3, 1)
    do(last_hop, 0, 1)
    lower(1, 0, RIGHT)
    do(add_opp, 3, 0)
    do(last_hop, 1, 1)
    multiply(2, 1)
    do(add_opp, 1, 0)
    do(add_opp, 0, 0)
    multiply(0, 1)
    multiply(1, 1)
    lower(0, 1, OPP)
    lower(3, 0, RIGHT)
    do(add_opp, 2, 0)
    lower(3, 1, OPP)
    lower(3, 0, LEFT)
    lower(2, 0, LEFT)
    lower(0, 1, LEFT)
    lower(2, 1, OPP)
    do(add_opp, 0, 1)
    lower(1, 1, OWN)
    lower(2, 1, RIGHT)
    lower(0, 0, OWN)
    do(add_side, 3, 0, RIGHT)
    do(add_side, 3, 0, LEFT)
    lower(1, 1, OPP)
    lower(0, 1, RIGHT)
    lower(3, 1, RIGHT)
    do(add_opp, 3, 1)
    lower(0, 0, RIGHT)
    lower(0, 1, OWN)
    lower(2, 1, LEFT)
    do(add_opp, 2, 1)
    lower(0, 0, LEFT)
    lower(1, 1, LEFT)
    lower(3, 1, LEFT)
    lower(3, 0, OWN)
    lower(3, 1, OWN)
    do(add_side, 0, 1, RIGHT)
    do(add_side, 0, 1, LEFT)
    do(add_side, 0, 0, RIGHT)
    do(add_side, 0, 0, LEFT)
    do(add_side, 3, 1, RIGHT)
    do(add_side, 3, 1, LEFT)
    lower(2, 0, RIGHT)
    lower(2, 0, OWN)
    do(add_own, 3, 0)
    do(add_opp, 1, 1)
    lower(2, 1, OWN)
    lower(1, 0, LEFT)
    do(add_own, 0, 1)
    lower(1, 1, RIGHT)
    do(add_side, 2, 1, LEFT)
    do(add_side, 2, 1, RIGHT)
    do(add_side, 2, 0, LEFT)
    do(add_own, 0, 0)
    do(add_side, 2, 0, RIGHT)
    do(add_own, 3, 1)
    do(turn_back, 0)
    do(add_side, 1, 1, LEFT)
    do(add_side, 1, 1, RIGHT)
    do(add_own, 2, 1)
    do(add_side, 1, 0, LEFT)
    lower(1, 0, OWN)
    do(add_side, 1, 0, RIGHT)
    do(add_own, 2, 0)
    do(turn_back, 3)
    do(add_own, 1, 1)
    do(turn_back, 2)
    do(add_own, 1, 0)
    do(mix, 0)
    do(mix, 3)
    do(turn_back, 1)
    do(mix, 2)
    pl.when(c == 1)(take_middle)
    do(mix, 1)

    def all_sent(j):
        z_sent(*to_z, j)
        z_sent(*back_z, j)
        for d in range(1, NY):
            y_copy(j, d).wait_send()
            ry_copy(j, d).wait_send()
        for q in range(NY):
            for way in range(3):
                x_copy(j, q, way).wait_send()
        for h in range(2):
            for kind in range(4):
                c_copy(j, h, kind).wait_send()
                rx_copy(j, h, kind).wait_send()
                if j < FIRST - 1:
                    rc_copy(j, h, kind).wait_send()

    for j in range(FIRST):
        do(all_sent, j)
    pl.when(c == 0)(lambda: mid_copy.wait_send())

    def extras_sent():
        for h in range(2):
            for kind in range(4):
                rc_copy(FIRST - 1, h, kind).wait_send()

    pl.when(c == 1)(extras_sent)


def on_device(tokens, expert_ids, routing_weights, up_weight, down_weight):
    count, width = tokens.shape
    hidden = up_weight.shape[2]
    dma = pltpu.SemaphoreType.DMA
    blocks = (BLOCKS, BROWS, LANES)
    any_space = pl.BlockSpec(memory_space=pl.ANY)
    in_vmem = pl.BlockSpec(memory_space=pltpu.VMEM)
    per_z, per_y = dma((FIRST, NZ)), dma((FIRST, NY))
    by_way, by_kind = dma((FIRST, 3 * NY)), dma((FIRST, 8))
    tile_set = pltpu.VMEM((FIRST,) + blocks, BF16)
    kind_set = pltpu.VMEM((FIRST, 4) + blocks, BF16)
    return pl.pallas_call(
        kernel,
        out_shape=jax.ShapeDtypeStruct((width // (NX * NC), count), BF16),
        in_specs=[any_space] * 5,
        out_specs=in_vmem,
        scratch_shapes=[
            pltpu.VMEM((TOP, count), jnp.int32),
            pltpu.VMEM((TOP, count), F32),
            pltpu.VMEM((FIRST, count, LANES), BF16),
            pltpu.VMEM(up_weight.shape, BF16),
            pltpu.VMEM(down_weight.shape, BF16),
            pltpu.VMEM((ROWS, count), BF16),
            pltpu.VMEM((ROWS, ROWS), BF16),
            pltpu.VMEM((ROWS, 2 * count), BF16),
            tile_set,
            tile_set,
            tile_set,
            pltpu.VMEM((NX * TILES,) + blocks, BF16),
            pltpu.VMEM((2, LOCAL, ROWS // LOCAL // 2, hidden), F32),
            pltpu.VMEM((2, LOCAL, ROWS // LOCAL // 2, hidden), BF16),
            kind_set,
            pltpu.VMEM((FIRST - 1, 4) + blocks, BF16),
            kind_set,
            pltpu.VMEM((FIRST, 2, 2, LOCAL, BROWS, LANES), BF16),
            pltpu.VMEM((FIRST, 2) + blocks, BF16),
            tile_set,
            tile_set,
            tile_set,
            tile_set,
            pltpu.VMEM((LANES // 2, count), BF16),
            pltpu.VMEM((LANES // 2, count), BF16),
            dma((FIRST,)),
            dma((4,)),
            per_z, per_z, per_y, per_y, by_way, by_way, by_kind, by_kind,
            by_kind, by_kind, by_kind, by_kind, per_y, per_y, per_z, per_z, dma, dma,
        ],
        compiler_params=pltpu.CompilerParams(
            collective_id=0, has_side_effects=True, vmem_limit_bytes=52 * 1024 * 1024
        ),
        cost_estimate=pl.CostEstimate(
            flops=4 * ROWS * width * hidden, bytes_accessed=8 * width * hidden, transcendentals=0
        ),
        name="experts",
    )(expert_ids.T, routing_weights.T, tokens, up_weight, down_weight).T


def solution(mesh):
    placed = (P("ep", None), P("ep", None), P("ep", None), P("ep", None, "tp"), P("ep", "tp", None))
    return jax.shard_map(
        on_device, mesh=mesh, in_specs=placed, out_specs=P("ep", "tp"), check_vma=False
    )
```

time: 100 us -> 83.4 us (0.83)
  Pallas kernels: 98.2 us -> 80.6 us
    pallas_call x1, Pallas kernels: 98.2 us -> 80.6 us  [on_device(): pl.pallas_call(kernel, out_shape=jax.ShapeDtypeStruct((width // (NX * NC)...]
    unnamed x0 -> x5, local copies, waits for them, and re-layouts: none -> 2.05 us
    pallas_call x1 -> x0, local copies, waits for them, and re-layouts: 1.78 us -> none  [on_device(): pl.pallas_call(kernel, out_shape=jax.ShapeDtypeStruct((count, width // (N...]
where the time goes in v3:
time: 83.4 us; the launch traced here: 82.7 us
  Pallas kernels  80.6 us (97%)
  local copies, waits for them, and re-layouts  2.05 us (2%)
    pallas_call x1, Pallas kernels, on_device(): pl.pallas_call(kernel, out_shape=jax.ShapeDtypeStruct((width // (NX * NC)...  80.6 us
    unnamed x5, local copies, waits for them, and re-layouts  2.05 us

profile of v3, /device:TPU:2, one launch (start us, length us, event | category | flops | bytes accessed | tf_op | source)
XLA Modules:
  0.0 82.7 jit_solution(7389490216919555447)
XLA Ops:
  0.0 0.0 copy-start
  0.0 0.7 copy-done
  0.7 0.0 copy-start.1
  0.7 0.7 copy-done.1
  1.4 80.6 %experts.1 = bf16[448,256]{1,0:T(8,128)(2,1)S(1)} custom-call(s32[2,256]{1,0:T(2,128)S(1)} %bitcast.4, f32[2,256]{1,0:T(2,128)S(1)} %bitcast.5, bf16[256,3584]{1,0:T(8,128)(2,1)} %tok_hbm.1, bf16[2,3584,384]{2,1,0:T(8,128)(2,1)} %up_hbm.1, bf16[2,384,3584]{2,1,0:T(8,128)(2,1)} %down_hbm.1), custom_call_target="tpu_custom_call" | custom-call | flops 3523215360 | bytes 11010048 | tf_op jit(solution)/shard_map/experts/pallas_call | solution.py:609
  82.0 0.7 copy.7
Async XLA Ops:
  0.0 0.7 copy-start
  0.7 0.7 copy-start.1

commit v4 on v3

--- a/solution.py
+++ b/solution.py
@@ -21,15 +21,18 @@
 ROWS = BLOCKS * BROWS
 HALF = BLOCKS // 2
 OPP, RIGHT, LEFT, OWN = 0, 1, 2, 3
-FIRST_UP, LAST_UP = (3, 3), (1, 1)
+FIRST_OUT = (2, 1)
+OVER_Z = (0, 3,)
+FIRST_UP, LAST_UP = (2, 2), (0, 1)
 
 
 def kernel(
     ids_hbm, rw_hbm, tok_hbm, up_hbm, down_hbm, out_ref,
     ids_ref, rw_ref, tok, up, down, place, perm, mixw,
-    gz, zb, yb, xb, raised, hid,
+    tok2, gz2, zb2, yb2, gz, zb, yb, xb, raised, hid,
     part, other, cross, half_in, full_in, summed, yr, zo, zr, mid_in, mid_out,
     tok_sem, w_sem,
+    tok2_sem, zs2, zr2, ys2, yr2,
     zs, zr_sem, ys, yr_sem, xs, xr, cs, cr,
     rcs, rcr, rxs, rxr, rys, ryr, rzs, rzr, ms, mr,
 ):
@@ -86,8 +89,15 @@
     def tok_copy(j):
         return pltpu.make_async_copy(tok_hbm.at[:, lanes(tile(x, j, c))], tok.at[j], tok_sem.at[j])
 
-    for j in range(FIRST):
+    def tok2_copy(j):
+        return pltpu.make_async_copy(
+            tok_hbm.at[:, lanes(tile(opp, j, c))], tok2.at[j], tok2_sem.at[j]
+        )
+
+    for j in FIRST_OUT + tuple(j for j in range(FIRST) if j not in FIRST_OUT):
         owned(j, lambda j=j: tok_copy(j).start())
+    for j in OVER_Z:
+        owned(j, lambda j=j: tok2_copy(j).start())
     up_copy = pltpu.make_async_copy(up_hbm, up, w_sem.at[0])
     down_copy = pltpu.make_async_copy(down_hbm, down, w_sem.at[1])
     up_copy.start()
@@ -114,6 +124,14 @@
         hits = jnp.where(at == pos0, 1.0, 0.0) + jnp.where(at == pos1, 1.0, 0.0)
         place[b * BROWS:(b + 1) * BROWS, :] = hits.astype(BF16)
 
+    def fill(j):
+        tok_copy(j).wait()
+        rows = jnp.dot(place[...], tok[j], preferred_element_type=F32)
+        gz[j] = rows.astype(BF16).reshape(BLOCKS, BROWS, LANES)
+
+    for j in FIRST_OUT:
+        owned(j, lambda j=j: fill(j))
+
     pl.semaphore_wait(barrier, (NZ - 1) + (NY - 1) + 3)
 
     def z_copy(src, dst, send, recv, j, d):
@@ -197,10 +215,32 @@
         return push(dst, dst, cs.at[j, 4 * h + kind], cr.at[j, 4 * h + kind], ep, tp)
 
     def gather(j):
-        tok_copy(j).wait()
-        rows = jnp.dot(place[...], tok[j], preferred_element_type=F32)
-        gz[j] = as_blocks(rows.astype(BF16))
+        if j not in FIRST_OUT:
+            fill(j)
         z_start(*to_z, j)
+
+    to_z2 = (gz2, zb2, zs2, zr2)
+
+    def y2_copy(j, d):
+        to = lax.rem(y + d, NY)
+        return push(
+            yb2.at[j, y_rows(to)], xb.at[tile(opp, j, c), quarter(d)], ys2.at[j, d], yr2.at[j, d],
+            z * NY + to, tp,
+        )
+
+    def gather2(j):
+        tok2_copy(j).wait()
+        rows = jnp.dot(place[...], tok2[j], preferred_element_type=F32)
+        gz2[j] = as_blocks(rows.astype(BF16))
+        z_start(*to_z2, j)
+
+    def turn2(j):
+        z_wait(*to_z2, j)
+        rows = jnp.dot(perm[...], as_rows(zb2[j]), preferred_element_type=F32)
+        yb2[j] = as_blocks(rows.astype(BF16))
+        for d in (2, 1, 3):
+            y2_copy(j, d).start()
+        xb[tile(opp, j, c), quarter(0)] = yb2[j, y_rows(y)]
 
     def spread(j, q):
         x_copy(j, q, 0).start()
@@ -223,7 +263,8 @@
 
     def forward(j, q):
         x_land(j, q, q % 2).wait_recv()
-        x_copy(j, q, 2).start()
+        if j not in OVER_Z:
+            x_copy(j, q, 2).start()
 
     def pass_left(j, h):
         x_land(j, 2 * h + 1, 0).wait_recv()
@@ -234,8 +275,12 @@
         c_copy(j, h, RIGHT).start()
 
     def last_hop(j, h):
-        x_land(j, 2 * h, 2).wait_recv()
-        x_land(j, 2 * h + 1, 2).wait_recv()
+        if j in OVER_Z:
+            for d in ((1,), (2, 3))[h]:
+                y2_copy(j, d).wait_recv()
+        else:
+            x_land(j, 2 * h, 2).wait_recv()
+            x_land(j, 2 * h + 1, 2).wait_recv()
         c_copy(j, h, OPP).start()
 
     def multiply(j, h):
@@ -421,160 +466,168 @@
     def do(step, j, *h):
         owned(j, lambda: step(j, *h))
 
+    do(gather, 2)
+    make_perm()
+    do(gather, 1)
     do(gather, 3)
+    do(turn, 2)
     do(gather, 0)
-    do(gather, 2)
-    do(gather, 1)
-    make_perm()
+    do(turn, 1)
+    do(forward, 2, 0)
+    do(side, 2, 1)
+    do(side, 2, 3)
+    do(gather2, 3)
+    do(side, 2, 2)
+    do(gather2, 0)
     do(turn, 3)
-    do(turn, 0)
-    do(side, 3, 3)
-    do(side, 3, 1)
-    do(side, 3, 2)
-    do(turn, 2)
-    do(side, 0, 3)
-    do(side, 0, 2)
-    do(side, 0, 1)
-    do(turn, 1)
-    do(side, 2, 1)
-    do(forward, 0, 0)
-    do(side, 2, 3)
-    do(forward, 0, 1)
-    do(forward, 3, 1)
-    do(forward, 3, 0)
-    do(pass_left, 0, 0)
-    do(side, 2, 2)
     do(side, 1, 1)
-    do(pass_left, 3, 0)
     do(side, 1, 3)
     do(forward, 2, 1)
-    do(forward, 2, 0)
+    do(turn, 0)
+    do(forward, 2, 2)
+    do(side, 3, 1)
+    do(turn2, 3)
+    do(side, 3, 3)
+    do(forward, 1, 0)
+    do(forward, 2, 3)
+    do(pass_right, 2, 0)
+    do(pass_left, 2, 1)
+    do(forward, 3, 0)
+    do(pass_left, 2, 0)
     do(side, 1, 2)
-    do(pass_right, 2, 0)
+    do(forward, 1, 1)
+    do(forward, 0, 0)
+    do(side, 0, 1)
+    do(turn2, 0)
+    do(pass_left, 3, 0)
+    do(side, 0, 3)
+    do(last_hop, 2, 0)
+    do(pass_right, 2, 1)
+    do(forward, 3, 3)
+    do(side, 3, 2)
+    do(forward, 3, 1)
+    do(pass_right, 1, 0)
+    do(last_hop, 2, 1)
     do(last_hop, 3, 0)
-    do(forward, 1, 0)
-    do(forward, 1, 1)
+    do(pass_right, 3, 0)
+    do(side, 0, 2)
+    do(pass_left, 1, 0)
+    up_copy.wait()
+    multiply(2, 0)
+    do(forward, 1, 3)
+    do(forward, 1, 2)
+    do(last_hop, 1, 0)
+    multiply(2, 1)
+    do(forward, 0, 1)
+    do(pass_right, 1, 1)
     do(pass_right, 0, 0)
+    do(pass_left, 0, 0)
+    multiply(3, 0)
+    do(last_hop, 0, 0)
+    multiply(1, 0)
     do(forward, 3, 2)
-    do(forward, 3, 3)
-    make_mix()
-    do(forward, 2, 2)
-    do(forward, 2, 3)
-    do(pass_left, 2, 0)
-    do(pass_right, 3, 0)
+    do(pass_left, 1, 1)
+    do(pass_right, 3, 1)
+    do(pass_left, 3, 1)
+    do(last_hop, 3, 1)
+    do(forward, 0, 3)
     do(forward, 0, 2)
-    do(last_hop, 0, 0)
+    do(last_hop, 0, 1)
+    do(pass_right, 0, 1)
     do(pass_left, 0, 1)
-    do(pass_right, 3, 1)
-    do(forward, 0, 3)
-    do(pass_right, 0, 1)
-    do(forward, 1, 3)
-    do(pass_left, 3, 1)
-    do(pass_left, 1, 0)
-    do(pass_right, 1, 0)
-    do(pass_left, 2, 1)
-    do(last_hop, 2, 0)
-    up_copy.wait()
-    multiply(3, 0)
-    do(forward, 1, 2)
-    do(pass_right, 1, 1)
-    do(last_hop, 1, 0)
-    do(pass_right, 2, 1)
     multiply(0, 0)
-    multiply(2, 0)
-    do(last_hop, 3, 1)
-    do(pass_left, 1, 1)
-    multiply(1, 0)
     down_copy.wait()
-    lower(3, 0, OPP)
-    do(last_hop, 2, 1)
     lower(0, 0, OPP)
+    lower(2, 0, OPP)
     lower(1, 0, OPP)
-    lower(2, 0, OPP)
+    do(last_hop, 1, 1)
     multiply(3, 1)
-    do(last_hop, 0, 1)
-    lower(1, 0, RIGHT)
-    do(add_opp, 3, 0)
-    do(last_hop, 1, 1)
-    multiply(2, 1)
-    do(add_opp, 1, 0)
     do(add_opp, 0, 0)
     multiply(0, 1)
+    do(add_opp, 1, 0)
     multiply(1, 1)
     lower(0, 1, OPP)
+    do(add_opp, 2, 0)
+    lower(3, 1, RIGHT)
+    lower(3, 1, OPP)
+    lower(3, 0, OPP)
+    lower(0, 0, LEFT)
+    do(add_opp, 0, 1)
+    lower(0, 0, RIGHT)
+    lower(0, 0, OWN)
+    do(add_opp, 3, 1)
+    lower(1, 0, RIGHT)
+    lower(0, 1, LEFT)
+    do(add_opp, 3, 0)
+    lower(0, 1, RIGHT)
+    do(add_side, 0, 0, LEFT)
+    lower(2, 1, OPP)
+    do(add_side, 0, 0, RIGHT)
+    lower(0, 1, OWN)
+    lower(3, 1, LEFT)
+    lower(1, 1, OPP)
+    lower(2, 1, OWN)
+    do(add_side, 0, 1, LEFT)
+    do(add_side, 0, 1, RIGHT)
+    lower(2, 1, LEFT)
+    do(add_opp, 1, 1)
+    do(add_opp, 2, 1)
+    lower(2, 0, LEFT)
+    lower(2, 1, RIGHT)
+    lower(3, 0, LEFT)
+    lower(1, 1, RIGHT)
+    lower(2, 0, RIGHT)
+    lower(3, 0, OWN)
+    lower(1, 0, LEFT)
+    lower(1, 1, LEFT)
     lower(3, 0, RIGHT)
-    do(add_opp, 2, 0)
-    lower(3, 1, OPP)
-    lower(3, 0, LEFT)
-    lower(2, 0, LEFT)
-    lower(0, 1, LEFT)
-    lower(2, 1, OPP)
-    do(add_opp, 0, 1)
+    lower(3, 1, OWN)
+    do(add_side, 3, 1, LEFT)
+    lower(1, 0, OWN)
+    do(add_side, 3, 1, RIGHT)
     lower(1, 1, OWN)
-    lower(2, 1, RIGHT)
-    lower(0, 0, OWN)
+    do(add_side, 3, 0, LEFT)
     do(add_side, 3, 0, RIGHT)
-    do(add_side, 3, 0, LEFT)
-    lower(1, 1, OPP)
-    lower(0, 1, RIGHT)
-    lower(3, 1, RIGHT)
-    do(add_opp, 3, 1)
-    lower(0, 0, RIGHT)
-    lower(0, 1, OWN)
-    lower(2, 1, LEFT)
-    do(add_opp, 2, 1)
-    lower(0, 0, LEFT)
-    lower(1, 1, LEFT)
-    lower(3, 1, LEFT)
-    lower(3, 0, OWN)
-    lower(3, 1, OWN)
-    do(add_side, 0, 1, RIGHT)
-    do(add_side, 0, 1, LEFT)
-    do(add_side, 0, 0, RIGHT)
-    do(add_side, 0, 0, LEFT)
-    do(add_side, 3, 1, RIGHT)
-    do(add_side, 3, 1, LEFT)
-    lower(2, 0, RIGHT)
+    do(add_own, 0, 1)
+    do(add_own, 0, 0)
+    do(add_side, 1, 1, LEFT)
+    do(add_side, 1, 0, LEFT)
+    do(add_side, 1, 1, RIGHT)
     lower(2, 0, OWN)
+    do(add_side, 1, 0, RIGHT)
+    do(add_side, 2, 1, RIGHT)
+    do(add_own, 3, 1)
+    make_mix()
+    do(add_side, 2, 0, RIGHT)
     do(add_own, 3, 0)
-    do(add_opp, 1, 1)
-    lower(2, 1, OWN)
-    lower(1, 0, LEFT)
-    do(add_own, 0, 1)
-    lower(1, 1, RIGHT)
     do(add_side, 2, 1, LEFT)
-    do(add_side, 2, 1, RIGHT)
     do(add_side, 2, 0, LEFT)
-    do(add_own, 0, 0)
-    do(add_side, 2, 0, RIGHT)
-    do(add_own, 3, 1)
     do(turn_back, 0)
-    do(add_side, 1, 1, LEFT)
-    do(add_side, 1, 1, RIGHT)
-    do(add_own, 2, 1)
-    do(add_side, 1, 0, LEFT)
-    lower(1, 0, OWN)
-    do(add_side, 1, 0, RIGHT)
-    do(add_own, 2, 0)
     do(turn_back, 3)
     do(add_own, 1, 1)
+    do(add_own, 1, 0)
+    do(add_own, 2, 1)
+    do(add_own, 2, 0)
+    do(turn_back, 1)
+    do(mix, 3)
+    do(mix, 0)
     do(turn_back, 2)
-    do(add_own, 1, 0)
-    do(mix, 0)
-    do(mix, 3)
-    do(turn_back, 1)
-    do(mix, 2)
     pl.when(c == 1)(take_middle)
     do(mix, 1)
+    do(mix, 2)
 
     def all_sent(j):
         z_sent(*to_z, j)
         z_sent(*back_z, j)
+        if j in OVER_Z:
+            z_sent(*to_z2, j)
         for d in range(1, NY):
+            if j in OVER_Z:
+                y2_copy(j, d).wait_send()
             y_copy(j, d).wait_send()
             ry_copy(j, d).wait_send()
         for q in range(NY):
-            for way in range(3):
+            for way in range(2 if j in OVER_Z else 3):
                 x_copy(j, q, way).wait_send()
         for h in range(2):
             for kind in range(4):
@@ -620,6 +673,10 @@
             pltpu.VMEM((ROWS, count), BF16),
             pltpu.VMEM((ROWS, ROWS), BF16),
             pltpu.VMEM((ROWS, 2 * count), BF16),
+            pltpu.VMEM((FIRST, count, LANES), BF16),
+            tile_set,
+            tile_set,
+            tile_set,
             tile_set,
             tile_set,
             tile_set,
@@ -639,6 +696,7 @@
             pltpu.VMEM((LANES // 2, count), BF16),
             dma((FIRST,)),
             dma((4,)),
+            dma((FIRST,)), per_z, per_z, per_y, per_y,
             per_z, per_z, per_y, per_y, by_way, by_way, by_kind, by_kind,
             by_kind, by_kind, by_kind, by_kind, per_y, per_y, per_z, per_z, dma, dma,
         ],

time: 83.4 us -> 79.8 us (0.957)
  Pallas kernels: 80.6 us -> 76.4 us
    pallas_call x1, Pallas kernels: 80.6 us -> 76.4 us  [on_device(): pl.pallas_call(kernel, out_shape=jax.ShapeDtypeStruct((width // (NX * NC)...]
where the time goes in v4:
time: 79.8 us; the launch traced here: 78.5 us
  Pallas kernels  76.4 us (96%)
  local copies, waits for them, and re-layouts  2.05 us (3%)
    pallas_call x1, Pallas kernels, on_device(): pl.pallas_call(kernel, out_shape=jax.ShapeDtypeStruct((width // (NX * NC)...  76.4 us
    unnamed x5, local copies, waits for them, and re-layouts  2.05 us

profile of v4, /device:TPU:2, one launch (start us, length us, event | category | flops | bytes accessed | tf_op | source)
XLA Modules:
  0.0 78.5 jit_solution(5494370738268919006)
XLA Ops:
  0.0 0.0 copy-start
  0.0 0.7 copy-done
  0.7 0.0 copy-start.1
  0.7 0.7 copy-done.1
  1.4 76.4 %experts.1 = bf16[448,256]{1,0:T(8,128)(2,1)S(1)} custom-call(s32[2,256]{1,0:T(2,128)S(1)} %bitcast.4, f32[2,256]{1,0:T(2,128)S(1)} %bitcast.5, bf16[256,3584]{1,0:T(8,128)(2,1)} %tok_hbm.1, bf16[2,3584,384]{2,1,0:T(8,128)(2,1)} %up_hbm.1, bf16[2,384,3584]{2,1,0:T(8,128)(2,1)} %down_hbm.1), custom_call_target="tpu_custom_call" | custom-call | flops 3523215360 | bytes 11010048 | tf_op jit(solution)/shard_map/experts/pallas_call | solution.py:662
  77.8 0.7 copy.7
Async XLA Ops:
  0.0 0.7 copy-start
  0.7 0.7 copy-start.1

commit v5 on v4

--- a/solution.py
+++ b/solution.py
@@ -21,9 +21,10 @@
 ROWS = BLOCKS * BROWS
 HALF = BLOCKS // 2
 OPP, RIGHT, LEFT, OWN = 0, 1, 2, 3
+LATE = (0, 2)
 FIRST_OUT = (2, 1)
 OVER_Z = (0, 3,)
-FIRST_UP, LAST_UP = (2, 2), (0, 1)
+FIRST_UP, LAST_UP = (2, 2), (0, 0)
 
 
 def kernel(
@@ -466,159 +467,10 @@
     def do(step, j, *h):
         owned(j, lambda: step(j, *h))
 
-    do(gather, 2)
-    make_perm()
-    do(gather, 1)
-    do(gather, 3)
-    do(turn, 2)
-    do(gather, 0)
-    do(turn, 1)
-    do(forward, 2, 0)
-    do(side, 2, 1)
-    do(side, 2, 3)
-    do(gather2, 3)
-    do(side, 2, 2)
-    do(gather2, 0)
-    do(turn, 3)
-    do(side, 1, 1)
-    do(side, 1, 3)
-    do(forward, 2, 1)
-    do(turn, 0)
-    do(forward, 2, 2)
-    do(side, 3, 1)
-    do(turn2, 3)
-    do(side, 3, 3)
-    do(forward, 1, 0)
-    do(forward, 2, 3)
-    do(pass_right, 2, 0)
-    do(pass_left, 2, 1)
-    do(forward, 3, 0)
-    do(pass_left, 2, 0)
-    do(side, 1, 2)
-    do(forward, 1, 1)
-    do(forward, 0, 0)
-    do(side, 0, 1)
-    do(turn2, 0)
-    do(pass_left, 3, 0)
-    do(side, 0, 3)
-    do(last_hop, 2, 0)
-    do(pass_right, 2, 1)
-    do(forward, 3, 3)
-    do(side, 3, 2)
-    do(forward, 3, 1)
-    do(pass_right, 1, 0)
-    do(last_hop, 2, 1)
-    do(last_hop, 3, 0)
-    do(pass_right, 3, 0)
-    do(side, 0, 2)
-    do(pass_left, 1, 0)
-    up_copy.wait()
-    multiply(2, 0)
-    do(forward, 1, 3)
-    do(forward, 1, 2)
-    do(last_hop, 1, 0)
-    multiply(2, 1)
-    do(forward, 0, 1)
-    do(pass_right, 1, 1)
-    do(pass_right, 0, 0)
-    do(pass_left, 0, 0)
-    multiply(3, 0)
-    do(last_hop, 0, 0)
-    multiply(1, 0)
-    do(forward, 3, 2)
-    do(pass_left, 1, 1)
-    do(pass_right, 3, 1)
-    do(pass_left, 3, 1)
-    do(last_hop, 3, 1)
-    do(forward, 0, 3)
-    do(forward, 0, 2)
-    do(last_hop, 0, 1)
-    do(pass_right, 0, 1)
-    do(pass_left, 0, 1)
-    multiply(0, 0)
-    down_copy.wait()
-    lower(0, 0, OPP)
-    lower(2, 0, OPP)
-    lower(1, 0, OPP)
-    do(last_hop, 1, 1)
-    multiply(3, 1)
-    do(add_opp, 0, 0)
-    multiply(0, 1)
-    do(add_opp, 1, 0)
-    multiply(1, 1)
-    lower(0, 1, OPP)
-    do(add_opp, 2, 0)
-    lower(3, 1, RIGHT)
-    lower(3, 1, OPP)
-    lower(3, 0, OPP)
-    lower(0, 0, LEFT)
-    do(add_opp, 0, 1)
-    lower(0, 0, RIGHT)
-    lower(0, 0, OWN)
-    do(add_opp, 3, 1)
-    lower(1, 0, RIGHT)
-    lower(0, 1, LEFT)
-    do(add_opp, 3, 0)
-    lower(0, 1, RIGHT)
-    do(add_side, 0, 0, LEFT)
-    lower(2, 1, OPP)
-    do(add_side, 0, 0, RIGHT)
-    lower(0, 1, OWN)
-    lower(3, 1, LEFT)
-    lower(1, 1, OPP)
-    lower(2, 1, OWN)
-    do(add_side, 0, 1, LEFT)
-    do(add_side, 0, 1, RIGHT)
-    lower(2, 1, LEFT)
-    do(add_opp, 1, 1)
-    do(add_opp, 2, 1)
-    lower(2, 0, LEFT)
-    lower(2, 1, RIGHT)
-    lower(3, 0, LEFT)
-    lower(1, 1, RIGHT)
-    lower(2, 0, RIGHT)
-    lower(3, 0, OWN)
-    lower(1, 0, LEFT)
-    lower(1, 1, LEFT)
-    lower(3, 0, RIGHT)
-    lower(3, 1, OWN)
-    do(add_side, 3, 1, LEFT)
-    lower(1, 0, OWN)
-    do(add_side, 3, 1, RIGHT)
-    lower(1, 1, OWN)
-    do(add_side, 3, 0, LEFT)
-    do(add_side, 3, 0, RIGHT)
-    do(add_own, 0, 1)
-    do(add_own, 0, 0)
-    do(add_side, 1, 1, LEFT)
-    do(add_side, 1, 0, LEFT)
-    do(add_side, 1, 1, RIGHT)
-    lower(2, 0, OWN)
-    do(add_side, 1, 0, RIGHT)
-    do(add_side, 2, 1, RIGHT)
-    do(add_own, 3, 1)
-    make_mix()
-    do(add_side, 2, 0, RIGHT)
-    do(add_own, 3, 0)
-    do(add_side, 2, 1, LEFT)
-    do(add_side, 2, 0, LEFT)
-    do(turn_back, 0)
-    do(turn_back, 3)
-    do(add_own, 1, 1)
-    do(add_own, 1, 0)
-    do(add_own, 2, 1)
-    do(add_own, 2, 0)
-    do(turn_back, 1)
-    do(mix, 3)
-    do(mix, 0)
-    do(turn_back, 2)
-    pl.when(c == 1)(take_middle)
-    do(mix, 1)
-    do(mix, 2)
-
     def all_sent(j):
         z_sent(*to_z, j)
-        z_sent(*back_z, j)
+        if j not in LATE:
+            z_sent(*back_z, j)
         if j in OVER_Z:
             z_sent(*to_z2, j)
         for d in range(1, NY):
@@ -636,16 +488,168 @@
                 if j < FIRST - 1:
                     rc_copy(j, h, kind).wait_send()
 
-    for j in range(FIRST):
-        do(all_sent, j)
-    pl.when(c == 0)(lambda: mid_copy.wait_send())
-
     def extras_sent():
         for h in range(2):
             for kind in range(4):
                 rc_copy(FIRST - 1, h, kind).wait_send()
 
+
+    do(gather, 2)
+    do(gather, 1)
+    do(gather, 3)
+    make_perm()
+    do(turn, 2)
+    do(gather, 0)
+    do(turn, 1)
+    do(side, 2, 1)
+    do(side, 2, 3)
+    do(forward, 2, 0)
+    do(side, 2, 2)
+    do(gather2, 3)
+    do(gather2, 0)
+    do(turn, 3)
+    do(side, 1, 3)
+    do(forward, 2, 1)
+    do(side, 1, 1)
+    do(pass_left, 2, 0)
+    do(turn, 0)
+    do(side, 3, 1)
+    do(forward, 2, 3)
+    do(forward, 2, 2)
+    do(pass_right, 2, 0)
+    do(side, 1, 2)
+    do(turn2, 3)
+    do(forward, 3, 0)
+    do(side, 0, 1)
+    do(side, 3, 3)
+    do(forward, 1, 1)
+    do(side, 3, 2)
+    do(pass_left, 2, 1)
+    do(forward, 1, 0)
+    do(turn2, 0)
+    do(forward, 3, 1)
+    do(pass_right, 2, 1)
+    do(last_hop, 2, 0)
+    do(forward, 1, 3)
+    do(side, 0, 3)
+    do(forward, 1, 2)
+    do(last_hop, 2, 1)
+    do(last_hop, 3, 0)
+    do(pass_right, 1, 0)
+    do(pass_right, 1, 1)
+    do(pass_right, 3, 0)
+    do(side, 0, 2)
+    do(forward, 0, 0)
+    do(pass_left, 3, 0)
+    do(pass_left, 1, 1)
+    do(pass_left, 1, 0)
+    up_copy.wait()
+    multiply(2, 0)
+    do(forward, 0, 1)
+    do(pass_left, 0, 0)
+    do(last_hop, 1, 0)
+    do(forward, 3, 3)
+    do(forward, 3, 2)
+    do(pass_right, 3, 1)
+    do(pass_right, 0, 0)
+    multiply(2, 1)
+    do(pass_left, 3, 1)
+    do(last_hop, 0, 0)
+    do(last_hop, 3, 1)
+    multiply(3, 0)
+    multiply(1, 0)
+    do(last_hop, 1, 1)
+    multiply(0, 0)
+    down_copy.wait()
+    lower(1, 0, OPP)
+    do(forward, 0, 3)
+    lower(2, 0, OPP)
+    do(forward, 0, 2)
+    do(last_hop, 0, 1)
+    do(pass_right, 0, 1)
+    do(pass_left, 0, 1)
+    multiply(3, 1)
+    lower(0, 0, OPP)
+    do(add_opp, 1, 0)
+    multiply(1, 1)
+    do(add_opp, 2, 0)
+    multiply(0, 1)
+    lower(1, 1, OPP)
+    lower(3, 1, OPP)
+    do(add_opp, 0, 0)
+    lower(3, 1, OWN)
+    lower(2, 1, RIGHT)
+    lower(1, 0, RIGHT)
+    lower(3, 1, RIGHT)
+    lower(1, 0, LEFT)
+    do(add_opp, 3, 1)
+    do(add_opp, 1, 1)
+    lower(3, 0, OPP)
+    lower(1, 1, RIGHT)
+    lower(2, 1, OWN)
+    lower(1, 1, LEFT)
+    lower(2, 0, LEFT)
+    do(add_side, 1, 0, RIGHT)
+    lower(0, 0, RIGHT)
+    lower(0, 1, OPP)
+    do(add_opp, 3, 0)
+    do(add_side, 1, 0, LEFT)
+    lower(2, 1, LEFT)
+    lower(3, 0, LEFT)
+    lower(0, 1, RIGHT)
+    lower(1, 0, OWN)
+    lower(2, 1, OPP)
+    make_mix()
+    lower(0, 1, LEFT)
+    do(add_side, 1, 1, LEFT)
+    do(add_side, 1, 1, RIGHT)
+    lower(3, 1, LEFT)
+    do(add_opp, 0, 1)
+    do(add_side, 3, 1, LEFT)
+    lower(0, 0, OWN)
+    do(add_opp, 2, 1)
+    lower(1, 1, OWN)
+    do(add_side, 3, 0, LEFT)
+    do(add_side, 3, 1, RIGHT)
+    lower(3, 0, RIGHT)
+    do(add_own, 1, 0)
+    lower(0, 0, LEFT)
+    lower(2, 0, RIGHT)
+    lower(0, 1, OWN)
+    do(add_side, 3, 0, RIGHT)
+    do(add_own, 1, 1)
+    do(add_side, 0, 1, LEFT)
+    do(add_side, 0, 1, RIGHT)
+    lower(2, 0, OWN)
+    do(add_side, 0, 0, LEFT)
+    do(add_side, 0, 0, RIGHT)
+    lower(3, 0, OWN)
+    do(add_side, 2, 1, RIGHT)
+    do(add_own, 3, 1)
+    do(add_side, 2, 1, LEFT)
+    do(add_side, 2, 0, LEFT)
+    do(add_own, 3, 0)
+    do(add_side, 2, 0, RIGHT)
+    do(turn_back, 1)
+    do(turn_back, 3)
+    do(add_own, 0, 1)
+    do(add_own, 0, 0)
+    do(add_own, 2, 1)
+    do(add_own, 2, 0)
+    do(turn_back, 0)
+    do(mix, 3)
+    do(turn_back, 2)
+    pl.when(c == 1)(take_middle)
+    do(mix, 1)
+    do(mix, 0)
+    for j in range(FIRST):
+        do(all_sent, j)
     pl.when(c == 1)(extras_sent)
+    do(mix, 2)
+
+    for j in LATE:
+        do(lambda j: z_sent(*back_z, j), j)
+    pl.when(c == 0)(lambda: mid_copy.wait_send())
 
 
 def on_device(tokens, expert_ids, routing_weights, up_weight, down_weight):

time: 79.8 us -> 79.3 us (level)
  no operation moved by 1% of the time
where the time goes in v5:
time: 79.3 us; the launch traced here: 78.3 us
  Pallas kernels  76.2 us (96%)
  local copies, waits for them, and re-layouts  2.05 us (3%)
    pallas_call x1, Pallas kernels, on_device(): pl.pallas_call(kernel, out_shape=jax.ShapeDtypeStruct((width // (NX * NC)...  76.2 us
    unnamed x5, local copies, waits for them, and re-layouts  2.05 us

profile of v5, /device:TPU:2, one launch (start us, length us, event | category | flops | bytes accessed | tf_op | source)
XLA Modules:
  0.0 78.3 jit_solution(16028035506088689655)
XLA Ops:
  0.0 0.0 copy-start
  0.0 0.7 copy-done
  0.7 0.0 copy-start.1
  0.7 0.7 copy-done.1
  1.4 76.2 %experts.1 = bf16[448,256]{1,0:T(8,128)(2,1)S(1)} custom-call(s32[2,256]{1,0:T(2,128)S(1)} %bitcast.4, f32[2,256]{1,0:T(2,128)S(1)} %bitcast.5, bf16[256,3584]{1,0:T(8,128)(2,1)} %tok_hbm.1, bf16[2,3584,384]{2,1,0:T(8,128)(2,1)} %up_hbm.1, bf16[2,384,3584]{2,1,0:T(8,128)(2,1)} %down_hbm.1), custom_call_target="tpu_custom_call" | custom-call | flops 3523215360 | bytes 11010048 | tf_op jit(solution)/shard_map/experts/pallas_call | solution.py:666
  77.6 0.7 copy.7
Async XLA Ops:
  0.0 0.7 copy-start
  0.7 0.7 copy-start.1

commit v6 on v4

--- a/solution.py
+++ b/solution.py
@@ -21,6 +21,7 @@
 ROWS = BLOCKS * BROWS
 HALF = BLOCKS // 2
 OPP, RIGHT, LEFT, OWN = 0, 1, 2, 3
+LATE = (1, 2)
 FIRST_OUT = (2, 1)
 OVER_Z = (0, 3,)
 FIRST_UP, LAST_UP = (2, 2), (0, 1)
@@ -465,6 +466,33 @@
 
     def do(step, j, *h):
         owned(j, lambda: step(j, *h))
+
+    def all_sent(j):
+        z_sent(*to_z, j)
+        if j not in LATE:
+            z_sent(*back_z, j)
+        if j in OVER_Z:
+            z_sent(*to_z2, j)
+        for d in range(1, NY):
+            if j in OVER_Z:
+                y2_copy(j, d).wait_send()
+            y_copy(j, d).wait_send()
+            ry_copy(j, d).wait_send()
+        for q in range(NY):
+            for way in range(2 if j in OVER_Z else 3):
+                x_copy(j, q, way).wait_send()
+        for h in range(2):
+            for kind in range(4):
+                c_copy(j, h, kind).wait_send()
+                rx_copy(j, h, kind).wait_send()
+                if j < FIRST - 1:
+                    rc_copy(j, h, kind).wait_send()
+
+    def extras_sent():
+        for h in range(2):
+            for kind in range(4):
+                rc_copy(FIRST - 1, h, kind).wait_send()
+
 
     do(gather, 2)
     make_perm()
@@ -614,38 +642,14 @@
     do(turn_back, 2)
     pl.when(c == 1)(take_middle)
     do(mix, 1)
-    do(mix, 2)
-
-    def all_sent(j):
-        z_sent(*to_z, j)
-        z_sent(*back_z, j)
-        if j in OVER_Z:
-            z_sent(*to_z2, j)
-        for d in range(1, NY):
-            if j in OVER_Z:
-                y2_copy(j, d).wait_send()
-            y_copy(j, d).wait_send()
-            ry_copy(j, d).wait_send()
-        for q in range(NY):
-            for way in range(2 if j in OVER_Z else 3):
-                x_copy(j, q, way).wait_send()
-        for h in range(2):
-            for kind in range(4):
-                c_copy(j, h, kind).wait_send()
-                rx_copy(j, h, kind).wait_send()
-                if j < FIRST - 1:
-                    rc_copy(j, h, kind).wait_send()
-
     for j in range(FIRST):
         do(all_sent, j)
+    pl.when(c == 1)(extras_sent)
+    do(mix, 2)
+
+    for j in LATE:
+        do(lambda j: z_sent(*back_z, j), j)
     pl.when(c == 0)(lambda: mid_copy.wait_send())
-
-    def extras_sent():
-        for h in range(2):
-            for kind in range(4):
-                rc_copy(FIRST - 1, h, kind).wait_send()
-
-    pl.when(c == 1)(extras_sent)
 
 
 def on_device(tokens, expert_ids, routing_weights, up_weight, down_weight):

time: 79.8 us -> 79.2 us (level)
  no operation moved by 1% of the time
where the time goes in v6:
time: 79.2 us; the launch traced here: 77.9 us
  Pallas kernels  75.8 us (96%)
  local copies, waits for them, and re-layouts  2.05 us (3%)
    pallas_call x1, Pallas kernels, on_device(): pl.pallas_call(kernel, out_shape=jax.ShapeDtypeStruct((width // (NX * NC)...  75.8 us
    unnamed x5, local copies, waits for them, and re-layouts  2.05 us

profile of v6, /device:TPU:2, one launch (start us, length us, event | category | flops | bytes accessed | tf_op | source)
XLA Modules:
  0.0 77.9 jit_solution(13611628206841247804)
XLA Ops:
  0.0 0.0 copy-start
  0.0 0.7 copy-done
  0.7 0.0 copy-start.1
  0.7 0.7 copy-done.1
  1.4 75.8 %experts.1 = bf16[448,256]{1,0:T(8,128)(2,1)S(1)} custom-call(s32[2,256]{1,0:T(2,128)S(1)} %bitcast.4, f32[2,256]{1,0:T(2,128)S(1)} %bitcast.5, bf16[256,3584]{1,0:T(8,128)(2,1)} %tok_hbm.1, bf16[2,3584,384]{2,1,0:T(8,128)(2,1)} %up_hbm.1, bf16[2,384,3584]{2,1,0:T(8,128)(2,1)} %down_hbm.1), custom_call_target="tpu_custom_call" | custom-call | flops 3523215360 | bytes 11010048 | tf_op jit(solution)/shard_map/experts/pallas_call | solution.py:666
  77.2 0.7 copy.7
Async XLA Ops:
  0.0 0.7 copy-start
  0.7 0.7 copy-start.1
